TPU v7x, 512 devices: a whole 4x4x16 slice. The times are simulated.
512 devices in a mesh: half: 2 (over core), face: 8 (over x, y_lo), tile: 32 (over y_hi, z).
Axes of the slice: x: 4, y: 4 (y_hi: 2, y_lo: 2; y = y_hi * 2 + y_lo), z: 16, core: 2. Of those that a mesh axis runs over, the one named last changes fastest.
Arguments:
- state: bfloat16 [2, 16, 32, 4096], P('half', None, 'face', 'tile'), may hold values from -6 to 6
- cotangent: bfloat16 [2, 16, 32, 4096], P('half', None, 'face', 'tile'), may hold values from -6 to 6
- block_peer: int32 [2, 8, 32, 32, 1], P('half', 'face', 'tile'), may hold values from 0 to 31; in each aligned block of 32 rows (0 to 31, 32 to 63, ..., all dimensions but the last counted through in order) at most 2 rows name the same one
- source_start: int32 [2, 8, 32, 32], P('half', 'face', 'tile'), may hold values from 0 to 448
- target_start: int32 [2, 8, 32, 32, 2], P('half', 'face', 'tile'), may hold values from 0 to 448
- interp: bfloat16 [2, 64, 64], P('half'), may hold values from -0.75 to 0.75
- sea_mask: int32 [2, 32, 4096], P('half', 'face', 'tile'), may hold values 0 or 1
- w_first: bfloat16 [2, 9, 1280], P('half'), may hold values from -0.4375 to 0.4375
- w_down: bfloat16 [2, 9, 8192], P('half'), may hold values from -0.25 to 0.25
- w_up: bfloat16 [2, 9, 12288], P('half'), may hold values from -0.15625 to 0.15625
- w_out: bfloat16 [2, 1024], P('half'), may hold values from -0.75 to 0.75
Outputs:
- predicted: bfloat16 [2, 16, 32, 4096], P('half', None, 'face', 'tile')
- grad_first: float32 [2, 9, 1280], P('half')
- grad_down: float32 [2, 9, 8192], P('half')
- grad_up: float32 [2, 9, 12288], P('half')
- grad_out: float32 [2, 1024], P('half')
Inputs may be any that keep to these rules, and one draw needn't show every extreme that they name: `block_peer`: of the blocks of one device no more than 2 name the same tile, and in every draw some device has exactly 2 blocks to one tile. `target_start`: entries of slots that no block uses are never read.
All inputs are finite; a program needn't handle non-finite values. No bound on the sum of `sea_mask` on one device may be relied on, other than what follows from the above.
Results may differ from a plain program's by a relative error of at most 0.0082.
Values may be sent and summed in bfloat16 or wider, within the bound.
A program may use at most 64 MiB of HBM per device.

v0:
```python
import math

import jax
import jax.numpy as jnp
from jax import lax
from jax.sharding import PartitionSpec as P

CH = 64
CIN = 16
KC = 4
BS = 64
CAP = 2


GELU_C = math.sqrt(2.0 / math.pi)


def extended(block, sides, width):
    for axis, dim in sides:
        count = lax.axis_size(axis)
        forward = [(i, i + 1) for i in range(count - 1)]
        backward = [(target, source) for source, target in forward]
        low = lax.ppermute(
            lax.slice_in_dim(block, block.shape[dim] - width, None, axis=dim), axis, forward
        )
        high = lax.ppermute(lax.slice_in_dim(block, 0, width, axis=dim), axis, backward)
        block = jnp.concatenate([low, block, high], axis=dim)
    return block


def swapped(block, axis, bit):
    count = lax.axis_size(axis)
    route = []
    for low in range(count):
        high = low | 1 << bit
        if high != low and high < count:
            route += [(low, high), (high, low)]
    return lax.ppermute(block, axis, route)


def gelu_value(pre):
    inner = jnp.tanh(GELU_C * (pre + 0.044715 * pre * pre * pre))
    return 0.5 * pre * (1.0 + inner)


def gelu_slope(pre):
    inner = jnp.tanh(GELU_C * (pre + 0.044715 * pre * pre * pre))
    return 0.5 * (1.0 + inner) + 0.5 * pre * (1.0 - inner * inner) * GELU_C * (
        1.0 + 3.0 * 0.044715 * pre * pre
    )


def spread(field):
    return extended(field, (("face", 1), ("tile", 2)), 1)


def convolve(padded, weight, height, breadth):
    chans = padded.shape[0]
    result = jnp.zeros((weight.shape[1], height * breadth), jnp.float32)
    for kernel_pos in range(9):
        row_shift, col_shift = (kernel_pos // 3, kernel_pos % 3)
        window = padded[:, row_shift : row_shift + height, col_shift : col_shift + breadth].reshape(
            chans, -1
        )
        result = result + jnp.dot(weight[kernel_pos], window, preferred_element_type=jnp.float32)
    return result


def convolve_adjoint(padded, weight, height, breadth):
    chans = padded.shape[0]
    result = jnp.zeros((weight.shape[2], height * breadth), jnp.float32)
    for kernel_pos in range(9):
        row_shift, col_shift = (kernel_pos // 3, kernel_pos % 3)
        window = padded[
            :, 2 - row_shift : 2 - row_shift + height, 2 - col_shift : 2 - col_shift + breadth
        ].reshape(chans, -1)
        result = result + lax.dot_general(
            weight[kernel_pos], window, (((0,), (0,)), ((), ())), preferred_element_type=jnp.float32
        )
    return result


def weight_grad(delta, padded, height, breadth):
    chans = padded.shape[0]
    parts = []
    for kernel_pos in range(9):
        row_shift, col_shift = (kernel_pos // 3, kernel_pos % 3)
        window = padded[:, row_shift : row_shift + height, col_shift : col_shift + breadth].reshape(
            chans, -1
        )
        parts.append(
            lax.dot_general(
                delta, window, (((1,), (1,)), ((), ())), preferred_element_type=jnp.float32
            )
        )
    return jnp.stack(parts)


def pool_pairs(field):
    chans, height, breadth = field.shape
    return (
        field.astype(jnp.float32)
        .reshape(chans, height // 2, 2, breadth // 2, 2)
        .mean(axis=(2, 4))
        .astype(jnp.bfloat16)
    )


def widen(field):
    return jnp.repeat(jnp.repeat(field, 2, axis=1), 2, axis=2)


def group_sum(field):
    chans, height, breadth = field.shape
    return field.reshape(chans, height // 2, 2, breadth // 2, 2).sum(axis=(2, 4))


def add_slots(running, arrived, offsets, matrix):
    moved = jnp.einsum("mckx,xy->mcky", arrived, matrix, preferred_element_type=jnp.float32)
    target_idx = offsets[..., None] + jnp.arange(BS, dtype=jnp.int32)
    return running.at[:, target_idx].add(jnp.transpose(moved, (2, 0, 1, 3)))


def local(
    state,
    cotangent,
    block_peer,
    source_start,
    target_start,
    interp,
    sea_mask,
    w_first,
    w_down,
    w_up,
    w_out,
):
    state_tile = state[0]
    tile_rows, tile_cols = (state_tile.shape[1], state_tile.shape[2])
    num_cells = tile_rows * tile_cols
    tile_count = lax.axis_size("tile")
    my_tile = lax.axis_index("tile")
    first_w = w_first[0].reshape(9, CH, CIN + KC)
    down_w = w_down[0].reshape(9, 2 * CH, CH)
    up_w = w_up[0].reshape(9, CH, 3 * CH)
    out_w = w_out[0].reshape(CIN, CH)
    export = state_tile[:KC].reshape(KC, num_cells)
    peer_ids = block_peer[0, 0, 0, :, 0]
    source_idx = source_start[0, 0, 0][:, None] + jnp.arange(BS, dtype=jnp.int32)[None, :]
    values = jnp.transpose(export[:, source_idx], (1, 0, 2))
    onehot = (peer_ids[:, None] == jnp.arange(tile_count, dtype=jnp.int32)[None, :]).astype(
        jnp.int32
    )
    slot_ids = jnp.sum(jnp.cumsum(onehot, axis=0) * onehot, axis=1) - 1
    outbox = jnp.zeros((tile_count, CAP, KC, BS), jnp.bfloat16).at[peer_ids, slot_ids].set(values)
    outbox = swapped(outbox, "half", 0)
    landing = target_start[0, 0, 0]
    matrix = interp[0]
    zero_sum = jnp.zeros((KC, num_cells), jnp.float32)
    arrived = lax.dynamic_index_in_dim(
        lax.all_gather(outbox[None], "tile", axis=0, tiled=True), my_tile, 1, keepdims=False
    )
    forcing_sum = add_slots(zero_sum, arrived, landing, matrix)
    sea_cells = sea_mask[0].reshape(1, num_cells).astype(jnp.float32)
    forcing = (forcing_sum * sea_cells).astype(jnp.bfloat16).reshape(KC, tile_rows, tile_cols)
    lifted_pad = spread(jnp.concatenate([state_tile, forcing], axis=0))
    pre_one = convolve(lifted_pad, first_w, tile_rows, tile_cols)
    hidden_one = gelu_value(pre_one).astype(jnp.bfloat16).reshape(CH, tile_rows, tile_cols)
    pooled_pad = spread(pool_pairs(hidden_one))
    pre_two = convolve(pooled_pad, down_w, tile_rows // 2, tile_cols // 2)
    hidden_two = (
        gelu_value(pre_two).astype(jnp.bfloat16).reshape(2 * CH, tile_rows // 2, tile_cols // 2)
    )
    joined_pad = spread(jnp.concatenate([hidden_one, widen(hidden_two)], axis=0))
    pre_three = convolve(joined_pad, up_w, tile_rows, tile_cols)
    hidden_three = gelu_value(pre_three).astype(jnp.bfloat16)
    base = state_tile.reshape(CIN, -1).astype(jnp.float32)
    predicted = (base + jnp.dot(out_w, hidden_three, preferred_element_type=jnp.float32)).astype(
        jnp.bfloat16
    )
    upstream = cotangent[0].reshape(CIN, -1)
    grad_out = lax.dot_general(
        upstream, hidden_three, (((1,), (1,)), ((), ())), preferred_element_type=jnp.float32
    )
    back_three = lax.dot_general(
        out_w, upstream, (((0,), (0,)), ((), ())), preferred_element_type=jnp.float32
    )
    d_three = (back_three * gelu_slope(pre_three)).astype(jnp.bfloat16)
    grad_up = weight_grad(d_three, joined_pad, tile_rows, tile_cols)
    d_join = convolve_adjoint(
        spread(d_three.reshape(CH, tile_rows, tile_cols)), up_w, tile_rows, tile_cols
    )
    back_two = group_sum(d_join[CH:].reshape(2 * CH, tile_rows, tile_cols)).reshape(2 * CH, -1)
    d_two = (back_two * gelu_slope(pre_two)).astype(jnp.bfloat16)
    grad_down = weight_grad(d_two, pooled_pad, tile_rows // 2, tile_cols // 2)
    d_pool = convolve_adjoint(
        spread(d_two.reshape(2 * CH, tile_rows // 2, tile_cols // 2)),
        down_w,
        tile_rows // 2,
        tile_cols // 2,
    )
    back_one = d_join[:CH] + 0.25 * widen(
        d_pool.reshape(CH, tile_rows // 2, tile_cols // 2)
    ).reshape(CH, -1)
    d_one = (back_one * gelu_slope(pre_one)).astype(jnp.bfloat16)
    grad_first = weight_grad(d_one, lifted_pad, tile_rows, tile_cols)
    scale = float(num_cells * lax.axis_size("face") * tile_count) ** (-0.5)
    flat_first = (grad_first * scale).reshape(9, -1)
    flat_down = (grad_down * scale).reshape(9, -1)
    flat_up = (grad_up * scale).reshape(9, -1)
    flat_out = (grad_out * scale).reshape(-1)
    flat_first, flat_down, flat_up, flat_out = lax.psum(
        (flat_first, flat_down, flat_up, flat_out), ("face", "tile")
    )
    return (
        predicted.reshape(1, CIN, tile_rows, tile_cols),
        flat_first[None],
        flat_down[None],
        flat_up[None],
        flat_out[None],
    )


def solution(mesh):
    return jax.shard_map(
        local,
        mesh=mesh,
        in_specs=(
            P("half", None, "face", "tile"),
            P("half", None, "face", "tile"),
            P("half", "face", "tile", None, None),
            P("half", "face", "tile", None),
            P("half", "face", "tile", None, None),
            P("half", None, None),
            P("half", "face", "tile"),
            P("half", None, None),
            P("half", None, None),
            P("half", None, None),
            P("half", None),
        ),
        out_specs=(
            P("half", None, "face", "tile"),
            P("half", None, None),
            P("half", None, None),
            P("half", None, None),
            P("half", None),
        ),
        check_vma=False,
    )
```

profile of v0, /device:TPU:0, one launch (start us, length us, event | category | flops | bytes accessed | tf_op | source)
XLA Modules:
  0.0 1685.5 jit_solution(14702500525758200464)
XLA Ops:
  7.2 0.7 fusion.56
  8.0 0.8 select_reduce_fusion
  8.8 0.7 fusion.61
  9.5 0.7 slice.380
  10.4 0.7 compare_select_fusion.1
  11.2 6.2 gather_fusion
  17.4 0.3 copy.57
  17.7 1.8 scatter_fusion
  19.6 1.9 collective-permute-start
  21.5 1.2 collective-permute-done
  22.7 0.6 copy-done.4
  23.4 0.8 copy.55
  24.4 0.7 convert_bitcast_fusion
  25.1 147.7 %all-gather.3.cloned.1.call-done = bf16[1024,2,4,64]{3,2,1,0:T(4,128)(2,1)} async-done(((bf16[32,2,4,64]{3,2,1,0:T(4,128)(2,1)}), bf16[1024,2,4,64]{3,2,1,0:T(4,128)(2,1)}) %all-gather.3.cloned.1.call-update) | async-done | bytes 1048592 | tf_op jit(solution)/shard_map/all_gather | solution.py:160
  172.8 0.9 constant_dynamic-slice_fusion
  173.8 0.7 copy.107
  174.6 22.4 %scatter_custom_fusion.1 = f32[4,512]{0,1:T(8,128)S(1)} fusion(s32[4096]{0:T(1024)S(1)} %reshape.522, f32[4096,4]{1,0:T(8,128)S(1)} %bitcast.337, f32[]{:T(128)} %constant.15.clone.1), kind=kCustom, calls=%fused_computation.87 | custom fusion | flops 16384 | bytes 8196 | tf_op jit(solution)/shard_map/scatter-add | solution.py:121
  197.2 2.5 collective-permute-start.1
  199.7 1.3 collective-permute-start.2
  202.1 3.5 collective-permute-done.2
  205.7 3.4 collective-permute-start.3
  209.2 1.3 collective-permute-start.4
  211.0 4.1 collective-permute-done.4
  217.3 4.8 collective-permute-start.5
  222.1 1.4 collective-permute-start.6
  223.6 0.8 slice_reduce_fusion.10
  225.3 2.6 collective-permute-done.6
  227.9 2.5 collective-permute-start.7
  230.4 1.3 collective-permute-start.8
  231.9 4.0 collective-permute-done.8
  237.5 1.3 collective-permute-start.10
  238.8 4.5 collective-permute-start.9
  243.3 1.2 slice_reduce_fusion.1
  245.6 3.4 collective-permute-start.11
  249.0 1.5 collective-permute-start.12
  250.9 3.7 collective-permute-done.12
  254.6 0.3 maximum_maximum_fusion
  255.9 0.3 convolution_add_fusion.11
  257.7 0.3 fusion.13
  259.7 0.8 stack.119
  260.6 3.9 collective-permute-start.13
  264.6 1.3 collective-permute-start.14
  266.1 4.9 collective-permute-done.14
  271.3 1.3 collective-permute-start.15
  272.7 1.1 broadcast_in_dim.49
  273.9 0.6 reshape.483
  274.5 4.5 collective-permute-start.16
  279.1 0.7 pad_maximum_fusion.15
  280.1 1.5 collective-permute-done.16
  281.6 0.7 pad_maximum_fusion.11
  282.3 0.3 convolution_add_fusion.7
  282.8 0.3 convolution_add_fusion.5
  287.4 4.8 collective-permute-start.17
  292.2 1.3 collective-permute-start.18
  293.5 0.4 stack.109
  294.0 0.9 multiply_bitcast_fusion
  294.9 3.0 collective-permute-done.18
  297.9 1.3 collective-permute-start.19
  299.2 5.0 collective-permute-start.20
  304.4 1.1 collective-permute-done.20
  310.0 1364.1 %all-reduce = (f32[1,9,1280]{2,1,0:T(8,128)S(1)}, f32[1,1024]{1,0:T(1,128)}) all-reduce(f32[1,9,1280]{2,1,0:T(8,128)S(1)} %multiply_bitcast_fusion.1, f32[1,1024]{1,0:T(1,128)S(1)} %broadcast_in_dim.50), channel_id=1, replica_groups=mesh['half'=2,'face'=8,'tile'=32] {'face','tile'}, use_global_device_ids=true, to_apply=%region_6.7 | all-reduce | flops 12544 | bytes 100352 | tf_op jit(solution)/shard_map/psum | solution.py:211
  1674.1 0.7 copy.86
  1674.8 2.1 copy.87
  1676.8 1.8 copy.179
  (231 shorter events, 23.0 us)
Async XLA Ops:
  7.2 166.5 %copy-start = (bf16[1,64,64]{2,1,0:T(8,128)(2,1)S(1)}, bf16[1,64,64]{2,1,0:T(8,128)(2,1)}, u32[]{:S(2)}) copy-start(bf16[1,64,64]{2,1,0:T(8,128)(2,1)} %param.16) | copy-start | bytes 24580
  7.2 165.6 %all-gather.3.cloned.1.call-start = ((), (), s32[]{:S(2)}) async-start(), calls=%async_computation | async-start | bytes 2162688 | tf_op jit(solution)/shard_map/all_gather | solution.py:160
  17.4 179.7 %copy-start.1 = (bf16[1,16,4,128]{3,2,1,0:T(4,128)(2,1)S(1)}, bf16[1,16,4,128]{3,2,1,0:T(4,128)(2,1)}, u32[]{:S(2)}) copy-start(bf16[1,16,4,128]{3,2,1,0:T(4,128)(2,1)} %param.11) | copy-start | bytes 49156
  17.4 183.5 %copy-start.5 = (bf16[1,9,1280]{2,1,0:T(8,128)(2,1)S(1)}, bf16[1,9,1280]{2,1,0:T(8,128)(2,1)}, u32[]{:S(2)}) copy-start(bf16[1,9,1280]{2,1,0:T(8,128)(2,1)} %param.18) | copy-start | bytes 69124
  19.6 3.1 collective-permute-start
  22.7 0.6 copy-start.4
  23.4 1651.4 %all-reduce.4.cloned.1.call-start = ((), (), s32[]{:S(2)}) async-start(), calls=%async_computation.1 | async-start | bytes 1933312 | tf_op jit(solution)/shard_map/psum | solution.py:211
  197.2 4.9 collective-permute-start.1
  199.7 5.9 collective-permute-start.2
  205.7 5.1 collective-permute-start.3
  209.2 5.9 collective-permute-start.4
  215.4 8.2 copy-start.3
  217.3 8.0 collective-permute-start.5
  222.1 21.2 %copy-start.2 = (bf16[1,9,12288]{2,1,0:T(8,128)(2,1)S(1)}, bf16[1,9,12288]{2,1,0:T(8,128)(2,1)}, u32[]{:S(2)}) copy-start(bf16[1,9,12288]{2,1,0:T(8,128)(2,1)} %param.20) | copy-start | bytes 663556
  222.1 5.8 collective-permute-start.6
  227.9 4.0 collective-permute-start.7
  230.4 5.5 collective-permute-start.8
  231.9 13.6 copy-start.7
  237.5 8.1 collective-permute-start.10
  238.8 6.8 collective-permute-start.9
  245.6 5.3 collective-permute-start.11
  249.0 5.5 collective-permute-start.12
  255.2 1.6 copy-start.6
  260.6 5.5 collective-permute-start.13
  264.6 6.5 collective-permute-start.14
  271.3 7.8 collective-permute-start.15
  274.5 7.0 collective-permute-start.16
  287.4 7.4 collective-permute-start.17
  292.2 5.6 collective-permute-start.18
  297.9 6.5 collective-permute-start.19
  299.2 6.3 collective-permute-start.20
Sparse Core Ops, SparseCore 0:
  23.5 149.2 all-gather.2
  295.0 406.5 all-reduce.3
where the time goes:
time: 1690 us
  blocking collectives  1360 us (80%)
  waiting for transfers between devices  178 us (11%)
  starting transfers between devices  54.6 us (3%)
  other arithmetic  30.6 us (2%)
  local copies, waits for them, and re-layouts  29.2 us (2%)
    psum x1, blocking collectives, local(): lax.psum((flat_first, flat_down, flat_up, flat_out), ('face', 'tile'))  1360 us
    all_gather x1, waiting for transfers between devices, local(): lax.all_gather(outbox[None], 'tile', axis=0, tiled=True)  148 us
    ppermute x10, starting transfers between devices, extended(): lax.ppermute(lax.slice_in_dim(block, block.shape[dim] - width, None, axis...  39.4 us
  transfers between devices with their start and end apart: 23, of which 13 were waited for; matrix products, arithmetic and copies ran while one was open for 1% of the time, Pallas kernels for 0%

commit v1 on v0

v1 whole, which is shorter than its diff:
```python
import functools
import math

import jax
import jax.numpy as jnp
import numpy as np
from jax import lax
from jax.experimental import pallas as pl
from jax.experimental.pallas import tpu as pltpu
from jax.sharding import PartitionSpec as P

CH = 64
CIN = 16
KC = 4
BS = 64
LANES = 128
GELU_C = math.sqrt(2.0 / math.pi)
BF = jnp.bfloat16
F32 = jnp.float32
MESH = pl.DeviceIdType.MESH
DIRS = [(-1, 0), (1, 0), (0, -1), (0, 1), (-1, -1), (-1, 1), (1, -1), (1, 1)]
OPP = [DIRS.index((-a, -b)) for a, b in DIRS]
N_EX = 5
EX_CH = (32, 128, 128, 64, 128)


def gelu_pair(pre):
    inner = jnp.tanh(GELU_C * (pre + 0.044715 * pre * pre * pre))
    value = 0.5 * pre * (1.0 + inner)
    slope = 0.5 * (1.0 + inner) + 0.5 * pre * (1.0 - inner * inner) * GELU_C * (
        1.0 + 3.0 * 0.044715 * pre * pre
    )
    return value, slope


def roll(x, shift):
    return pltpu.roll(x, shift % LANES, axis=1)


def lanes_of(rows):
    return lax.broadcasted_iota(jnp.int32, (rows, LANES), 1)


def barrel(x, amount, right):
    for bit in range(7):
        step = 1 << bit
        moved = roll(x, step if right else LANES - step)
        x = jnp.where((amount & step) != 0, moved, x)
    return x


def pair_sum(x):
    even = (lanes_of(x.shape[0]) & 1) == 0
    return x + jnp.where(even, roll(x, -1), roll(x, 1))


def edge_tables():
    pick_fine = np.zeros((16, 4 * LANES), np.float32)
    pick_coarse = np.zeros((16, 2 * LANES), np.float32)
    for base, lane in ((0, LANES - 1), (8, 0)):
        for j, row in enumerate((3, 0, 1, 2, 3, 0)):
            pick_fine[base + j, row * LANES + lane] = 1
            pick_coarse[base + j, (row // 2) * LANES + lane] = 1
    place_fine = np.zeros((3, 16, LANES), np.float32)
    place_coarse = np.zeros((3, 16, LANES), np.float32)
    for a in range(3):
        for base, start in ((0, 0), (8, 64)):
            for r in range(4):
                place_fine[a, base + r + a, start + r] = 1
            for r in range(2):
                place_coarse[a, base + (0, 1, 3, 5)[r + a], start + r] = 1
    return pick_fine, pick_coarse, place_fine, place_coarse


def conv_rows(weight, x_ref, outs, rows, step):
    z = jnp.dot(weight, x_ref[...], preferred_element_type=F32)
    lane = lanes_of(outs)
    halo_left = z[:outs, rows * LANES :]
    halo_right = z[2 * outs :, rows * LANES :]
    result = []
    for r in range(rows):
        at = slice(r * LANES, (r + 1) * LANES)
        left = jnp.where(lane < step, halo_left[:, r : r + 1], roll(z[:outs, at], step))
        right = jnp.where(
            lane >= LANES - step, halo_right[:, 64 + r : 65 + r], roll(z[2 * outs :, at], -step)
        )
        result.append(z[outs : 2 * outs, at] + left + right)
    return result


def weight_grad(delta_rows, x_ref, step):
    outs = delta_rows[0].shape[0]
    lane = lanes_of(outs)
    keep = (lane & (step - 1)) == 0
    zero = jnp.zeros((outs, LANES), F32)
    first, middle, last = [], [], []
    halo_left, halo_right = zero, zero
    for r, delta in enumerate(delta_rows):
        first.append(jnp.where(keep & (lane < LANES - step), roll(delta, -step), 0.0))
        middle.append(jnp.where(keep, delta, 0.0))
        last.append(jnp.where(keep & (lane >= step), roll(delta, step), 0.0))
        halo_left = jnp.where(lane == r, delta[:, 0:1], halo_left)
        halo_right = jnp.where(lane == 64 + r, delta[:, LANES - 1 : LANES], halo_right)
    parts = [first + [halo_left], middle + [zero], last + [halo_right]]
    stacked = jnp.concatenate(
        [jnp.concatenate(part, axis=1).astype(BF) for part in parts], axis=0
    )
    return lax.dot_general(
        stacked, x_ref[...], (((1,), (1,)), ((), ())), preferred_element_type=F32
    )


def kernel(
    nf,
    nt,
    na,
    nb,
    state_ref,
    cot_ref,
    peer_row_ref,
    peer_col_ref,
    src_ref,
    tgt_ref,
    interp_ref,
    sea_ref,
    a1_ref,
    a2_ref,
    a3_ref,
    b2_ref,
    b3_ref,
    wo_ref,
    wot_ref,
    pickf_ref,
    pickc_ref,
    placef_ref,
    placec_ref,
    pred_ref,
    ga_ref,
    gb_ref,
    outbox,
    inbox,
    row_send,
    row_recv,
    edge_send,
    edge_recv,
    x1,
    x2,
    x3,
    xd3,
    xd2,
    send_a,
    recv_a,
    part_a,
    zrecv_a,
    done_a,
    all_a,
    send_b,
    recv_b,
    part_b,
    zrecv_b,
    done_b,
    all_b,
    box_ssem,
    box_rsem,
    ex_ssem,
    ex_rsem,
    xy_ssem,
    xy_rsem,
    zs_ssem,
    zs_rsem,
    zg_ssem,
    zg_rsem,
    gx_ssem,
    gx_rsem,
):
    half = lax.axis_index("half")
    face = lax.axis_index("face")
    tile = lax.axis_index("tile")
    nz = nt // 2
    nxy = nf * 2
    y_hi = tile // nz
    z = tile % nz
    me_xy = face * 2 + y_hi

    def xy_peer(k):
        other = (me_xy + k) % nxy
        return other, {"face": other // 2, "tile": (other % 2) * nz + z}

    def z_peer(k):
        other = (z + k) % nz
        return other, {"tile": y_hi * nz + other}

    def box_peer(k):
        other = (tile + k) % nt
        return other, {"half": 1 - half, "tile": other}

    def neighbour(d):
        df, dt = DIRS[d]
        ok = (face + df >= 0) & (face + df < nf) & (tile + dt >= 0) & (tile + dt < nt)
        return ok, {"face": face + df, "tile": tile + dt}

    row_recv[...] = jnp.zeros_like(row_recv)
    edge_recv[...] = jnp.zeros_like(edge_recv)
    edge_send[...] = jnp.zeros_like(edge_send)

    barrier = pltpu.get_barrier_semaphore()

    def greet(peer, count):
        def body(k, carry):
            pl.semaphore_signal(barrier, inc=1, device_id=peer(k)[1], device_id_type=MESH)
            return carry

        lax.fori_loop(count[0], count[1], body, 0)

    greet(box_peer, (0, nt))
    greet(xy_peer, (1, nxy))
    greet(z_peer, (1, nz))
    expected = nt + nxy - 1 + nz - 1
    for d in range(8):
        ok, device = neighbour(d)
        expected = expected + ok.astype(jnp.int32)

        @pl.when(ok)
        def _(device=device):
            pl.semaphore_signal(barrier, inc=1, device_id=device, device_id_type=MESH)

    rows = 2 * nt * KC
    nblk = src_ref.shape[1]
    peer_row = peer_row_ref[...]
    same = peer_col_ref[...] == peer_row
    earlier = lax.broadcasted_iota(jnp.int32, (nblk, nblk), 0) < lax.broadcasted_iota(
        jnp.int32, (nblk, nblk), 1
    )
    rank = jnp.sum(jnp.where(same & earlier, 1.0, 0.0), axis=0, keepdims=True)
    row_id = lax.broadcasted_iota(jnp.int32, (rows, nblk), 0)
    slot = (row_id // (nt * KC)).astype(F32)
    match = ((row_id // KC) % nt == peer_row) & (slot == rank)
    used = jnp.sum(jnp.where(match, 1.0, 0.0), axis=1, keepdims=True)
    start = jnp.sum(
        jnp.where(match, src_ref[...].astype(F32), 0.0), axis=1, keepdims=True
    ).astype(jnp.int32)
    start = jnp.broadcast_to(start, (rows, LANES))
    lane = lanes_of(rows)
    sub8 = lax.broadcasted_iota(jnp.int32, (8, LANES), 0)
    shift = start & (LANES - 1)
    from_tile = (start >> 7) + (lane < shift).astype(jnp.int32)
    window = jnp.zeros((rows, LANES), F32)
    for q in range(4):
        head = state_ref[:, q * LANES : (q + 1) * LANES].astype(F32)[0:8]
        head = jnp.where(sub8 < KC, head, pltpu.roll(head, 4, axis=0))
        window = jnp.where(
            from_tile == q, jnp.concatenate([head] * (rows // 8), axis=0), window
        )
    window = barrel(window, shift, False)
    window = jnp.where((lane < BS) & (used > 0.0), window, 0.0)
    packed = window[: rows // 2] + roll(window[rows // 2 :], BS)
    for p in range(nt):
        outbox[p] = packed[p * KC : (p + 1) * KC]

    pl.semaphore_wait(barrier, expected)

    def box_copy(k):
        other, device = box_peer(k)
        return pltpu.make_async_remote_copy(
            src_ref=outbox.at[other],
            dst_ref=inbox.at[tile],
            send_sem=box_ssem.at[k],
            recv_sem=box_rsem.at[tile],
            device_id=device,
            device_id_type=MESH,
        )

    def box_arrival(k):
        other, device = box_peer(k)
        return pltpu.make_async_remote_copy(
            src_ref=outbox.at[other],
            dst_ref=inbox.at[other],
            send_sem=box_ssem.at[k],
            recv_sem=box_rsem.at[other],
            device_id=device,
            device_id_type=MESH,
        )

    def each(low, high, act):
        def body(k, carry):
            act(k)
            return carry

        lax.fori_loop(low, high, body, 0)

    each(0, nt, lambda k: box_copy(k).start())

    def ex_copy(e, d, arrival):
        ok, device = neighbour(d)
        at = d if arrival else OPP[d]
        if d < 2:
            src = row_send.at[e, d, 0 : EX_CH[e]]
            dst = row_recv.at[e, at, 0 : EX_CH[e]]
        else:
            src = edge_send.at[e]
            dst = edge_recv.at[e, at - 2]
        return ok, pltpu.make_async_remote_copy(
            src_ref=src,
            dst_ref=dst,
            send_sem=ex_ssem.at[e, d],
            recv_sem=ex_rsem.at[e, at],
            device_id=device,
            device_id_type=MESH,
        )

    def ex_start(e):
        for d in range(8):
            ok, copy = ex_copy(e, d, False)
            pl.when(ok)(copy.start)

    def ex_wait(e):
        for d in range(8):
            ok, copy = ex_copy(e, d, True)

            @pl.when(ok)
            def _(copy=copy):
                copy.wait_recv()
                copy.wait_send()

    def pick(table_ref, field):
        return lax.dot_general(
            table_ref[...], field, (((1,), (1,)), ((), ())), preferred_element_type=F32
        ).astype(BF)

    sub16 = lax.broadcasted_iota(jnp.int32, (16, LANES), 0)
    takes = {
        2: (sub16 >= 1) & (sub16 <= 4),
        3: (sub16 >= 9) & (sub16 <= 12),
        4: sub16 == 0,
        5: sub16 == 8,
        6: sub16 == 5,
        7: sub16 == 13,
    }

    def halo_columns(e):
        held = jnp.zeros((16, LANES), F32)
        for d in range(2, 8):
            held = jnp.where(takes[d], edge_recv[e, d - 2].astype(F32), held)
        return held.T

    def place(columns, table_ref, a):
        return jnp.dot(
            columns.astype(BF), table_ref[a], preferred_element_type=F32
        ).astype(BF)

    def fill_centre(x_ref, chans, offset, total, field_rows):
        count = len(field_rows)
        for a in range(3):
            for r in range(count):
                if 1 <= r + a <= count:
                    x_ref[
                        a * total + offset : a * total + offset + chans,
                        r * LANES : (r + 1) * LANES,
                    ] = field_rows[r + a - 1]

    def fill_halo(x_ref, chans, offset, total, count, above, below, columns, table_ref):
        x_ref[offset : offset + chans, 0:LANES] = above
        x_ref[
            2 * total + offset : 2 * total + offset + chans, (count - 1) * LANES : count * LANES
        ] = below
        for a in range(3):
            x_ref[
                a * total + offset : a * total + offset + chans, count * LANES :
            ] = place(columns, table_ref, a)

    def xy_copy(g, k, arrival):
        other, device = xy_peer(k)
        send, recv, m = ((send_a, recv_a, 16 * na), (send_b, recv_b, 16 * nb))[g]
        at = other if arrival else me_xy
        return pltpu.make_async_remote_copy(
            src_ref=send.at[pl.ds(pl.multiple_of(other * m, 16), m)],
            dst_ref=recv.at[at],
            send_sem=xy_ssem.at[g, k],
            recv_sem=xy_rsem.at[g, at],
            device_id=device,
            device_id_type=MESH,
        )

    groups = (
        (na, send_a, recv_a, part_a, zrecv_a, done_a, all_a, 0),
        (nb, send_b, recv_b, part_b, zrecv_b, done_b, all_b, 2),
    )

    def xy_start(g):
        each(1, nxy, lambda k: xy_copy(g, k, False).start())

    def z_owner(g, q):
        return (4 * q + groups[g][7]) % nz

    def zs_copy(g, q, source):
        n, send, recv, part, zrecv, done, full, first = groups[g]
        base = 0 if g == 0 else na
        return pltpu.make_async_remote_copy(
            src_ref=part.at[16 * q : 16 * q + 16],
            dst_ref=zrecv.at[q, source],
            send_sem=zs_ssem.at[base + q],
            recv_sem=zs_rsem.at[base + q, source],
            device_id={"tile": y_hi * nz + z_owner(g, q)},
            device_id_type=MESH,
        )

    def zg_copy(g, q, k):
        n, send, recv, part, zrecv, done, full, first = groups[g]
        base = 0 if g == 0 else na
        return pltpu.make_async_remote_copy(
            src_ref=done.at[16 * q : 16 * q + 16],
            dst_ref=done.at[16 * q : 16 * q + 16],
            send_sem=zg_ssem.at[base + q, k],
            recv_sem=zg_rsem.at[base + q],
            device_id=z_peer(k)[1],
            device_id_type=MESH,
        )

    def gx_copy(g, k, arrival):
        other, device = xy_peer(k)
        n, send, recv, part, zrecv, done, full, first = groups[g]
        m = 16 * n
        at = other if arrival else me_xy
        return pltpu.make_async_remote_copy(
            src_ref=done,
            dst_ref=full.at[pl.ds(pl.multiple_of(at * m, 16), m)],
            send_sem=gx_ssem.at[g, k],
            recv_sem=gx_rsem.at[g, at],
            device_id=device,
            device_id_type=MESH,
        )

    def stage_xy_to_z(g):
        n, send, recv, part, zrecv, done, full, first = groups[g]
        m = 16 * n
        total = send[pl.ds(pl.multiple_of(me_xy * m, 16), m), :].astype(F32)
        each(1, nxy, lambda k: xy_copy(g, k, True).wait_recv())
        recv[me_xy] = jnp.zeros((m, LANES), BF)
        for j in range(nxy):
            total = total + recv[j].astype(F32)
        part[...] = total.astype(BF)
        for q in range(n):

            @pl.when(z != z_owner(g, q))
            def _(q=q):
                zs_copy(g, q, z).start()

    def stage_z_reduce(g):
        n, send, recv, part, zrecv, done, full, first = groups[g]
        for q in range(n):

            @pl.when(z == z_owner(g, q))
            def _(q=q):
                each(1, nz, lambda k: zs_copy(g, q, z_peer(k)[0]).wait_recv())
                zrecv[q, z] = part[16 * q : 16 * q + 16]
                total = jnp.zeros((16, LANES), F32)
                for j in range(nz):
                    total = total + zrecv[q, j].astype(F32)
                done[16 * q : 16 * q + 16] = total.astype(BF)
                each(1, nz, lambda k: zg_copy(g, q, k).start())

    def stage_z_to_xy(g):
        n, send, recv, part, zrecv, done, full, first = groups[g]
        for q in range(n):

            @pl.when(z != z_owner(g, q))
            def _(q=q):
                zg_copy(g, q, 1).wait_recv()

        each(1, nxy, lambda k: gx_copy(g, k, False).start())

    def stage_finish(g, out_ref):
        n, send, recv, part, zrecv, done, full, first = groups[g]
        m = 16 * n
        each(1, nxy, lambda k: gx_copy(g, k, True).wait_recv())
        full[pl.ds(pl.multiple_of(me_xy * m, 16), m), :] = done[...]
        scale = 1.0 / math.sqrt(nf * 4 * nt * LANES)
        out_ref[...] = full[...].astype(F32) * scale
        each(1, nxy, lambda k: xy_copy(g, k, False).wait_send())
        for q in range(n):

            @pl.when(z != z_owner(g, q))
            def _(q=q):
                zs_copy(g, q, z).wait_send()

            @pl.when(z == z_owner(g, q))
            def _(q=q):
                each(1, nz, lambda k: zg_copy(g, q, k).wait_send())

        each(1, nxy, lambda k: gx_copy(g, k, False).wait_send())

    target = jnp.broadcast_to(tgt_ref[...], (rows, LANES))
    shift_in = target & (LANES - 1)
    to_tile = (target >> 7) + (lane < shift_in).astype(jnp.int32)
    each(0, nt, lambda k: box_arrival(k).wait_recv())
    arrived = jnp.concatenate([inbox[p] for p in range(nt)], axis=0)
    moved = jnp.dot(arrived.astype(BF), interp_ref[...], preferred_element_type=F32)
    lane_half = lanes_of(rows // 2)
    moved = jnp.concatenate(
        [
            jnp.where(lane_half < BS, moved, 0.0),
            roll(jnp.where(lane_half >= BS, moved, 0.0), BS),
        ],
        axis=0,
    )
    moved = barrel(moved, shift_in, True)
    lifted = []
    for q in range(4):
        chosen = jnp.where(to_tile == q, moved, 0.0)
        total = chosen[0:8]
        for i in range(1, rows // 8):
            total = total + chosen[8 * i : 8 * i + 8]
        total = total + pltpu.roll(total, 4, axis=0)
        total = total * sea_ref[q : q + 1, :].astype(F32)
        forcing = jnp.concatenate(
            [jnp.where(sub8 < KC, total, 0.0), jnp.zeros((8, LANES), F32)], axis=0
        ).astype(BF)
        lifted.append(
            jnp.concatenate([state_ref[:, q * LANES : (q + 1) * LANES], forcing], axis=0)
        )

    row_send[0, 0, 0:32] = lifted[0]
    row_send[0, 1, 0:32] = lifted[3]
    edge_send[0, :, 0:32] = pick(pickf_ref, jnp.concatenate(lifted, axis=1))
    ex_start(0)
    fill_centre(x1, 32, 0, 32, lifted)
    ex_wait(0)
    columns = halo_columns(0)[0:32]
    fill_halo(
        x1, 32, 0, 32, 4, row_recv[0, 0, 0:32], row_recv[0, 1, 0:32], columns, placef_ref
    )
    pre = conv_rows(a1_ref[...], x1, CH, 4, 1)
    hidden_one, slope_one = [], []
    for r in range(4):
        value, slope = gelu_pair(pre[r])
        hidden_one.append(value.astype(BF))
        slope_one.append(slope)
    pooled = [
        (
            pair_sum(hidden_one[2 * r].astype(F32) + hidden_one[2 * r + 1].astype(F32)) * 0.25
        ).astype(BF)
        for r in range(2)
    ]

    for at, fine, coarse in ((0, 0, 0), (1, 3, 1)):
        row_send[1, at, 0:CH] = hidden_one[fine]
        row_send[1, at, CH : 2 * CH] = pooled[coarse]
    edge_send[1] = jnp.concatenate(
        [
            pick(pickf_ref, jnp.concatenate(hidden_one, axis=1)),
            pick(pickc_ref, jnp.concatenate(pooled, axis=1)),
        ],
        axis=1,
    )
    ex_start(1)
    fill_centre(x3, CH, 0, 3 * CH, hidden_one)
    fill_centre(x2, CH, 0, CH, pooled)
    ex_wait(1)
    columns = halo_columns(1)
    fill_halo(
        x2,
        CH,
        0,
        CH,
        2,
        row_recv[1, 0, CH : 2 * CH],
        row_recv[1, 1, CH : 2 * CH],
        columns[CH : 2 * CH],
        placec_ref,
    )
    pre = conv_rows(a2_ref[...], x2, 2 * CH, 2, 2)
    hidden_two, slope_two = [], []
    for r in range(2):
        value, slope = gelu_pair(pre[r])
        hidden_two.append(value.astype(BF))
        slope_two.append(slope)

    row_send[2, 0] = hidden_two[0]
    row_send[2, 1] = hidden_two[1]
    edge_send[2] = pick(pickc_ref, jnp.concatenate(hidden_two, axis=1))
    ex_start(2)
    fill_halo(
        x3, CH, 0, 3 * CH, 4, row_recv[1, 0, 0:CH], row_recv[1, 1, 0:CH], columns[0:CH], placef_ref
    )
    fill_centre(x3, 2 * CH, CH, 3 * CH, [hidden_two[r // 2] for r in range(4)])
    back_three = jnp.dot(wot_ref[...], cot_ref[...], preferred_element_type=F32)
    ex_wait(2)
    columns = halo_columns(2)
    fill_halo(
        x3, 2 * CH, CH, 3 * CH, 4, row_recv[2, 0], row_recv[2, 1], columns, placef_ref
    )
    pre = conv_rows(a3_ref[...], x3, CH, 4, 1)
    hidden_three, delta_three = [], []
    for r in range(4):
        value, slope = gelu_pair(pre[r])
        hidden_three.append(value.astype(BF))
        delta_three.append(
            (back_three[:, r * LANES : (r + 1) * LANES] * slope).astype(BF)
        )

    row_send[3, 0, 0:CH] = delta_three[0]
    row_send[3, 1, 0:CH] = delta_three[3]
    edge_send[3, :, 0:CH] = pick(pickf_ref, jnp.concatenate(delta_three, axis=1))
    ex_start(3)
    fill_centre(xd3, CH, 0, CH, delta_three)
    flat_three = jnp.concatenate(hidden_three, axis=1)
    pred_ref[...] = (
        state_ref[...].astype(F32)
        + jnp.dot(wo_ref[...], flat_three, preferred_element_type=F32)
    ).astype(BF)
    grad_out = lax.dot_general(
        cot_ref[...], flat_three, (((1,), (1,)), ((), ())), preferred_element_type=F32
    )
    grad_up = weight_grad([d.astype(F32) for d in delta_three], x3, 1)
    for block in range(4):
        send_a[192 * block : 192 * block + 192] = grad_up[
            :, block * LANES : (block + 1) * LANES
        ].astype(BF)
    send_a[768:864] = jnp.concatenate([grad_up[0:96, 512:576], grad_up[96:192, 512:576]], axis=1).astype(BF)
    send_a[864:880] = jnp.concatenate([grad_out, jnp.zeros((16, 64), F32)], axis=1).astype(BF)
    if 16 * na * nxy > 880:
        send_a[880:] = jnp.zeros((16 * na * nxy - 880, LANES), BF)
    xy_start(0)
    ex_wait(3)
    columns = halo_columns(3)[0:CH]
    fill_halo(
        xd3, CH, 0, CH, 4, row_recv[3, 0, 0:CH], row_recv[3, 1, 0:CH], columns, placef_ref
    )
    join = conv_rows(b3_ref[...], xd3, 3 * CH, 4, 1)
    delta_two = [
        (pair_sum(join[2 * r][CH:] + join[2 * r + 1][CH:]) * slope_two[r]).astype(BF)
        for r in range(2)
    ]

    row_send[4, 0] = delta_two[0]
    row_send[4, 1] = delta_two[1]
    edge_send[4] = pick(pickc_ref, jnp.concatenate(delta_two, axis=1))
    ex_start(4)
    fill_centre(xd2, 2 * CH, 0, 2 * CH, delta_two)
    grad_down = weight_grad([d.astype(F32) for d in delta_two], x2, 2)
    send_b[0:384] = grad_down[:, 0:LANES].astype(BF)
    send_b[384:576] = jnp.concatenate([grad_down[0:192, 128:192], grad_down[192:384, 128:192]], axis=1).astype(BF)
    ex_wait(4)
    columns = halo_columns(4)
    fill_halo(
        xd2, 2 * CH, 0, 2 * CH, 2, row_recv[4, 0], row_recv[4, 1], columns, placec_ref
    )
    d_pool = conv_rows(b2_ref[...], xd2, CH, 2, 2)
    delta_one = [
        ((join[r][0:CH] + 0.25 * d_pool[r // 2]) * slope_one[r]).astype(BF).astype(F32)
        for r in range(4)
    ]
    grad_first = weight_grad(delta_one, x1, 1)
    send_b[576:768] = jnp.concatenate([grad_first, jnp.zeros((192, 32), F32)], axis=1).astype(BF)
    if 16 * nb * nxy > 768:
        send_b[768:] = jnp.zeros((16 * nb * nxy - 768, LANES), BF)
    xy_start(1)
    stage_xy_to_z(0)
    stage_xy_to_z(1)
    stage_z_reduce(0)
    stage_z_reduce(1)
    stage_z_to_xy(0)
    stage_z_to_xy(1)
    stage_finish(0, ga_ref)
    stage_finish(1, gb_ref)
    each(0, nt, lambda k: box_copy(k).wait_send())


def local(
    nf,
    nt,
    state,
    cotangent,
    block_peer,
    source_start,
    target_start,
    interp,
    sea_mask,
    w_first,
    w_down,
    w_up,
    w_out,
):
    nxy, nz = nf * 2, nt // 2
    na, nb = -(-55 // nxy), -(-48 // nxy)
    nblk = source_start.shape[-1]
    flat_state = state.reshape(CIN, 4 * LANES)
    flat_cot = cotangent.reshape(CIN, 4 * LANES)
    peer = block_peer.reshape(nblk)
    target = jnp.repeat(target_start.reshape(nt, 2).T.reshape(2 * nt), KC)[:, None]
    zero = jnp.zeros((BS, BS), BF)
    matrix = interp[0]
    pair = jnp.concatenate(
        [jnp.concatenate([matrix, zero], 1), jnp.concatenate([zero, matrix], 1)], 0
    )
    first = jnp.pad(
        w_first.reshape(3, 3, CH, CIN + KC), ((0, 0), (0, 0), (0, 0), (0, 12))
    )
    down = w_down.reshape(3, 3, 2 * CH, CH)
    up = w_up.reshape(3, 3, CH, 3 * CH)
    a1 = first.transpose(1, 2, 0, 3).reshape(3 * CH, 96)
    a2 = down.transpose(1, 2, 0, 3).reshape(6 * CH, 3 * CH)
    a3 = up.transpose(1, 2, 0, 3).reshape(3 * CH, 9 * CH)
    b2 = down[::-1, ::-1].transpose(1, 3, 0, 2).reshape(3 * CH, 6 * CH)
    b3 = up[::-1, ::-1].transpose(1, 3, 0, 2).reshape(9 * CH, 3 * CH)
    wo = w_out.reshape(CIN, CH)
    tables = [jnp.asarray(table, BF) for table in edge_tables()]
    operands = (
        flat_state,
        flat_cot,
        peer[None, :],
        peer[:, None],
        source_start.reshape(1, nblk),
        target,
        pair,
        sea_mask.reshape(4, LANES),
        a1,
        a2,
        a3,
        b2,
        b3,
        wo,
        wo.T,
        *tables,
    )
    dma = pltpu.SemaphoreType.DMA
    scratch = [
        pltpu.VMEM((nt, KC, LANES), F32),
        pltpu.VMEM((nt, KC, LANES), F32),
        pltpu.VMEM((N_EX, 2, LANES, LANES), BF),
        pltpu.VMEM((N_EX, 2, LANES, LANES), BF),
        pltpu.VMEM((N_EX, 16, LANES), BF),
        pltpu.VMEM((N_EX, 6, 16, LANES), BF),
        pltpu.VMEM((96, 5 * LANES), BF),
        pltpu.VMEM((3 * CH, 3 * LANES), BF),
        pltpu.VMEM((9 * CH, 5 * LANES), BF),
        pltpu.VMEM((3 * CH, 5 * LANES), BF),
        pltpu.VMEM((6 * CH, 3 * LANES), BF),
    ]
    for n in (na, nb):
        scratch += [
            pltpu.VMEM((nxy * n * 16, LANES), BF),
            pltpu.VMEM((nxy, n * 16, LANES), BF),
            pltpu.VMEM((n * 16, LANES), BF),
            pltpu.VMEM((n, nz, 16, LANES), BF),
            pltpu.VMEM((n * 16, LANES), BF),
            pltpu.VMEM((nxy * n * 16, LANES), BF),
        ]
    scratch += [
        dma((nt,)),
        dma((nt,)),
        dma((N_EX, 8)),
        dma((N_EX, 8)),
        dma((2, nxy)),
        dma((2, nxy)),
        dma((na + nb,)),
        dma((na + nb, nz)),
        dma((na + nb, nz)),
        dma((na + nb,)),
        dma((2, nxy)),
        dma((2, nxy)),
    ]
    vmem = pl.BlockSpec(memory_space=pltpu.VMEM)
    predicted, sums_a, sums_b = pl.pallas_call(
        functools.partial(kernel, nf, nt, na, nb),
        out_shape=(
            jax.ShapeDtypeStruct((CIN, 4 * LANES), BF),
            jax.ShapeDtypeStruct((nxy * na * 16, LANES), F32),
            jax.ShapeDtypeStruct((nxy * nb * 16, LANES), F32),
        ),
        in_specs=[vmem] * len(operands),
        out_specs=(vmem, vmem, vmem),
        scratch_shapes=scratch,
        compiler_params=pltpu.CompilerParams(
            collective_id=0, has_side_effects=True, vmem_limit_bytes=40 * 2**20
        ),
    )(*operands)

    grad_up = jnp.concatenate(
        [sums_a[192 * i : 192 * i + 192] for i in range(4)]
        + [jnp.concatenate([sums_a[768:864, 0:64], sums_a[768:864, 64:128]], 0)],
        axis=1,
    )
    grad_down = jnp.concatenate(
        [sums_b[0:384], jnp.concatenate([sums_b[384:576, 0:64], sums_b[384:576, 64:128]], 0)],
        axis=1,
    )
    grad_first = sums_b[576:768, 0:96].reshape(3, CH, 3, 32)[..., : CIN + KC]
    return (
        predicted.reshape(1, CIN, 4, LANES),
        grad_first.transpose(2, 0, 1, 3).reshape(1, 9, -1),
        grad_down.reshape(3, 2 * CH, 3, CH).transpose(2, 0, 1, 3).reshape(1, 9, -1),
        grad_up.reshape(3, CH, 3, 3 * CH).transpose(2, 0, 1, 3).reshape(1, 9, -1),
        sums_a[864:880, 0:64].reshape(1, -1),
    )


def solution(mesh):
    return jax.shard_map(
        functools.partial(local, mesh.shape["face"], mesh.shape["tile"]),
        mesh=mesh,
        in_specs=(
            P("half", None, "face", "tile"),
            P("half", None, "face", "tile"),
            P("half", "face", "tile", None, None),
            P("half", "face", "tile", None),
            P("half", "face", "tile", None, None),
            P("half", None, None),
            P("half", "face", "tile"),
            P("half", None, None),
            P("half", None, None),
            P("half", None, None),
            P("half", None),
        ),
        out_specs=(
            P("half", None, "face", "tile"),
            P("half", None, None),
            P("half", None, None),
            P("half", None, None),
            P("half", None),
        ),
        check_vma=False,
    )
```

time: 1690 us -> 99.5 us (0.06)
  the two profiles are of different devices: /device:TPU:0 before, /device:TPU:4 now
where the time goes in v1:
time: 99.5 us; the launch traced here: 99 us
  Pallas kernels  81.9 us (82%)
  local copies, waits for them, and re-layouts  16 us (16%)
    pallas_call x1, Pallas kernels, local(): pl.pallas_call(functools.partial(kernel, nf, nt, na, nb), out_shape=(jax....  81.9 us
    unnamed x35, local copies, waits for them, and re-layouts  4.4 us

profile of v1, /device:TPU:4, one launch (start us, length us, event | category | flops | bytes accessed | tf_op | source)
XLA Modules:
  0.0 99.0 jit_solution(13347432239181490148)
XLA Ops:
  0.6 0.0 copy-start.13
  0.6 0.0 copy-start.14
  0.7 0.7 copy-done.14
  1.3 0.1 reshape.83
  1.4 0.0 copy-done.13
  1.4 0.1 reshape.93.wo_ref
  1.5 0.1 copy.52
  1.6 0.0 copy-start.5
  1.6 0.7 copy-done.5
  2.3 0.1 copy.53.peer_col_ref
  2.4 0.1 broadcast_in_dim.4
  2.4 0.6 copy-done.10
  3.1 0.1 fusion.2.interp_ref
  3.2 0.6 copy-done.11
  3.8 0.0 copy-done.12
  3.8 0.1 broadcast_in_dim_reshape.12.tgt_ref
  3.9 0.7 copy-done.9
  4.6 0.4 reshape.85
  5.0 0.0 copy-start.8
  5.0 0.1 copy.47
  5.2 0.0 copy-start.7
  5.2 0.1 reshape.86
  5.3 0.1 copy.55.a1_ref
  5.4 0.5 copy-done.8
  6.0 0.3 reshape.87
  6.2 0.0 copy-done.7
  6.3 0.4 reshape.89
  6.6 0.2 copy.50
  6.9 0.3 copy.51
  7.1 1.6 %rev.7 = bf16[3,3,64,192]{3,1,2,0:T(4,128)(2,1)S(1)} reverse(bf16[3,3,64,192]{3,1,2,0:T(4,128)(2,1)S(1)} %copy.51), dimensions={0,1} | reverse | bytes 442368 | tf_op jit(solution)/shard_map/rev | solution.py:705
  8.8 0.3 reshape.92
  9.0 0.2 copy.57.b3_ref
  9.2 0.3 copy.75
  9.5 0.3 reshape.90.a3_ref
  9.8 0.3 copy.66
  10.0 0.0 copy-start
  10.1 0.0 copy-start.1
  10.1 0.0 copy-start.2
  10.1 0.0 copy-start.3
  10.1 0.0 copy-start.4
  10.1 0.0 copy-start.6
  10.1 0.2 reshape.102.a2_ref
  10.4 0.4 copy-done
  10.8 0.0 copy-done.1
  10.8 0.0 copy-done.2
  10.8 0.0 copy-done.3
  10.8 0.0 copy-done.4
  10.8 0.0 copy-done.6
  10.8 81.9 %shard_map.182 = (bf16[16,512]{1,0:T(8,128)(2,1)S(1)}, f32[1024,128]{1,0:T(8,128)S(1)}, f32[768,128]{1,0:T(8,128)S(1)}) custom-call(bf16[16,512]{1,0:T(8,128)(2,1)S(1)} %get-tuple-element.26.state_ref, bf16[16,512]{1,0:T(8,128)(2,1)S(1)} %get-tuple-element.25.cot_ref, s32[1,32]{1,0:T(1,128)S(1)} %bitcast.53, s32[32,1]{1,0:T(8,128)S(1)} %copy.53.peer_col_ref, ...), custom_call_target="tpu_custom_call" | custom-call | tf_op jit(solution)/shard_map/pallas_call | solution.py:764
  92.7 0.6 reshape.94
  93.3 0.7 reshape.101
  94.0 0.1 copy.58
  94.1 0.1 reshape.95
  94.2 0.1 fusion.3
  94.3 0.2 copy.59
  94.5 0.9 reshape.103
  95.4 0.1 fusion.4
  95.5 0.1 copy.60
  95.7 0.1 reshape.97
  95.8 0.2 copy.61
  96.0 1.1 %reshape.104 = f32[1,9,8192]{2,0,1:T(1,128)} reshape(f32[3,3,128,64]{3,2,1,0:T(8,128)S(1)} %copy.61) | data formatting | bytes 589824 | tf_op jit(solution)/shard_map/reshape | solution.py:792
  97.2 0.3 reshape.99
  97.5 0.1 copy.62
  97.7 1.3 %reshape.105 = f32[1,9,12288]{2,0,1:T(1,128)} reshape(f32[3,3,64,192]{3,2,1,0:T(8,128)S(1)} %copy.62) | data formatting | bytes 884736 | tf_op jit(solution)/shard_map/reshape | solution.py:793
  (19 shorter events, 0.2 us)
Async XLA Ops:
  0.6 0.8 copy-start.13
  0.6 0.7 copy-start.14
  1.6 0.7 copy-start.5
  2.4 0.7 copy-start.10
  3.1 0.7 copy-start.11
  3.1 0.7 copy-start.12
  3.8 0.8 copy-start.9
  5.0 1.0 copy-start.8
  5.2 1.1 %copy-start.7 = (bf16[1,9,12288]{2,1,0:T(8,128)(2,1)S(1)}, bf16[1,9,12288]{2,1,0:T(8,128)(2,1)}, u32[]{:S(2)}) copy-start(bf16[1,9,12288]{2,1,0:T(8,128)(2,1)} %param.24) | copy-start | bytes 663556
  10.0 0.7 copy-start
  10.1 0.7 copy-start.1
  10.1 0.7 copy-start.2
  10.1 0.7 copy-start.3
  10.1 0.7 copy-start.4
  10.1 0.7 copy-start.6

commit v2 on v1

--- a/solution.py
+++ b/solution.py
@@ -72,6 +72,23 @@
     return pick_fine, pick_coarse, place_fine, place_coarse
 
 
+def weight_tables():
+    up = np.zeros((576, 288), np.float32)
+    down = np.zeros((1152, 576), np.float32)
+    for b in range(3):
+        for a in range(3):
+            k = 3 * (2 - a) + 2 - b
+            for o in range(CH):
+                up[(b * 3 + a) * CH + o, 8 * (o // 2) + k if k < 8 else 256 + o // 2] = 1
+            for o in range(2 * CH):
+                down[(b * 3 + a) * 2 * CH + o, 8 * (o // 2) + k if k < 8 else 512 + o // 2] = 1
+    wide = CIN + KC
+    lane = np.arange(CH * wide)
+    mask = (lane[None, :] // wide == np.arange(CH)[:, None]).astype(np.float32)
+    fold = (lane[:, None] % wide == np.arange(32)[None, :]).astype(np.float32)
+    return up, down, mask, fold
+
+
 def conv_rows(weight, x_ref, outs, rows, step):
     z = jnp.dot(weight, x_ref[...], preferred_element_type=F32)
     lane = lanes_of(outs)
@@ -115,28 +132,57 @@
     nt,
     na,
     nb,
+    nc,
+    state_hbm,
+    cot_hbm,
+    peer_hbm,
+    src_hbm,
+    tgt_hbm,
+    interp_hbm,
+    sea_hbm,
+    w1_hbm,
+    w2_hbm,
+    w3_hbm,
+    wo_hbm,
+    up_hbm,
+    down_hbm,
+    mask_hbm,
+    fold_hbm,
+    pickf_hbm,
+    pickc_hbm,
+    placef_hbm,
+    placec_hbm,
+    pred_ref,
+    ga_ref,
+    gb_ref,
+    gc_ref,
     state_ref,
     cot_ref,
-    peer_row_ref,
-    peer_col_ref,
+    peer_ref,
     src_ref,
     tgt_ref,
     interp_ref,
     sea_ref,
-    a1_ref,
-    a2_ref,
-    a3_ref,
-    b2_ref,
-    b3_ref,
+    w1_ref,
+    w2_ref,
+    w3_ref,
     wo_ref,
-    wot_ref,
+    up_ref,
+    down_ref,
+    mask_ref,
+    fold_ref,
     pickf_ref,
     pickc_ref,
     placef_ref,
     placec_ref,
-    pred_ref,
-    ga_ref,
-    gb_ref,
+    load_sem,
+    s2,
+    s3,
+    a1,
+    a2,
+    a3,
+    b2,
+    b3,
     outbox,
     inbox,
     row_send,
@@ -160,6 +206,12 @@
     zrecv_b,
     done_b,
     all_b,
+    send_c,
+    recv_c,
+    part_c,
+    zrecv_c,
+    done_c,
+    all_c,
     box_ssem,
     box_rsem,
     ex_ssem,
@@ -172,6 +224,8 @@
     zg_rsem,
     gx_ssem,
     gx_rsem,
+    za_ssem,
+    za_rsem,
 ):
     half = lax.axis_index("half")
     face = lax.axis_index("face")
@@ -199,6 +253,35 @@
         ok = (face + df >= 0) & (face + df < nf) & (tile + dt >= 0) & (tile + dt < nt)
         return ok, {"face": face + df, "tile": tile + dt}
 
+    loads = [
+        pltpu.make_async_copy(src, dst, load_sem.at[i])
+        for i, (src, dst) in enumerate(
+            (
+                (state_hbm, state_ref),
+                (peer_hbm, peer_ref),
+                (src_hbm, src_ref),
+                (w3_hbm, w3_ref),
+                (up_hbm, up_ref),
+                (w2_hbm, w2_ref),
+                (down_hbm, down_ref),
+                (w1_hbm, w1_ref),
+                (mask_hbm, mask_ref),
+                (fold_hbm, fold_ref),
+                (wo_hbm, wo_ref),
+                (tgt_hbm, tgt_ref),
+                (interp_hbm, interp_ref),
+                (sea_hbm, sea_ref),
+                (cot_hbm, cot_ref),
+                (pickf_hbm, pickf_ref),
+                (pickc_hbm, pickc_ref),
+                (placef_hbm, placef_ref),
+                (placec_hbm, placec_ref),
+            )
+        )
+    ]
+    for load in loads:
+        load.start()
+
     row_recv[...] = jnp.zeros_like(row_recv)
     edge_recv[...] = jnp.zeros_like(edge_recv)
     edge_send[...] = jnp.zeros_like(edge_send)
@@ -226,8 +309,16 @@
 
     rows = 2 * nt * KC
     nblk = src_ref.shape[1]
-    peer_row = peer_row_ref[...]
-    same = peer_col_ref[...] == peer_row
+    for load in loads[:3]:
+        load.wait()
+    state3 = state_ref[...].astype(F32)
+    state_rows = [state3[:, q, :] for q in range(4)]
+    peer_col = jnp.broadcast_to(peer_ref[...], (nblk, nblk))
+    diagonal = lax.broadcasted_iota(jnp.int32, (nblk, nblk), 0) == lax.broadcasted_iota(
+        jnp.int32, (nblk, nblk), 1
+    )
+    peer_row = jnp.sum(jnp.where(diagonal, peer_col, 0), axis=0, keepdims=True)
+    same = peer_col == peer_row
     earlier = lax.broadcasted_iota(jnp.int32, (nblk, nblk), 0) < lax.broadcasted_iota(
         jnp.int32, (nblk, nblk), 1
     )
@@ -246,7 +337,7 @@
     from_tile = (start >> 7) + (lane < shift).astype(jnp.int32)
     window = jnp.zeros((rows, LANES), F32)
     for q in range(4):
-        head = state_ref[:, q * LANES : (q + 1) * LANES].astype(F32)[0:8]
+        head = state_rows[q][0:8]
         head = jnp.where(sub8 < KC, head, pltpu.roll(head, 4, axis=0))
         window = jnp.where(
             from_tile == q, jnp.concatenate([head] * (rows // 8), axis=0), window
@@ -289,6 +380,68 @@
         lax.fori_loop(low, high, body, 0)
 
     each(0, nt, lambda k: box_copy(k).start())
+
+    for load in loads[3:]:
+        load.wait()
+    for j in range(CH // 2):
+        part = w3_ref[:, 384 * j : 384 * j + 384].astype(F32)
+        s3[8 * j : 8 * j + 8] = part[0:8]
+        s3[256 + j : 257 + j] = part[8:9]
+    for j in range(CH):
+        part = w2_ref[:, 128 * j : 128 * j + 128].astype(F32)
+        s2[8 * j : 8 * j + 8] = part[0:8]
+        s2[512 + j : 513 + j] = part[8:9]
+    taps = jnp.dot(up_ref[...], s3[...].astype(BF), preferred_element_type=F32)
+    odd = (lax.broadcasted_iota(jnp.int32, (576, 192), 0) & 1) == 1
+    taps = jnp.where(odd, taps[:, 192:384], taps[:, 0:192])
+    for b in range(3):
+        b3[192 * b : 192 * b + 192] = taps[192 * b : 192 * b + 192].T.astype(BF)
+        for a in range(3):
+            at = ((2 - b) * 3 + 2 - a) * CH
+            a3[CH * b : CH * b + CH, 192 * a : 192 * a + 192] = taps[at : at + CH].astype(BF)
+    taps = jnp.dot(down_ref[...], s2[...].astype(BF), preferred_element_type=F32)
+    odd = (lax.broadcasted_iota(jnp.int32, (1152, LANES), 0) & 1) == 1
+    taps = jnp.where(odd, roll(taps, CH), taps)
+    for b in range(3):
+        b2[CH * b : CH * b + CH] = taps[384 * b : 384 * b + 384].T[0:CH].astype(BF)
+        for a in range(3):
+            at = ((2 - b) * 3 + 2 - a) * 2 * CH
+            a2[2 * CH * b : 2 * CH * b + 2 * CH, CH * a : CH * a + CH] = taps[
+                at : at + 2 * CH, 0:CH
+            ].astype(BF)
+    flat_first = w1_ref[...].astype(F32)
+    for k in range(9):
+        spread = mask_ref[...].astype(F32) * flat_first[k : k + 1]
+        a1[CH * (k % 3) : CH * (k % 3) + CH, 32 * (k // 3) : 32 * (k // 3) + 32] = jnp.dot(
+            spread.astype(BF), fold_ref[...], preferred_element_type=F32
+        ).astype(BF)
+    wo32 = jnp.zeros((16, LANES), F32)
+    sub16 = lax.broadcasted_iota(jnp.int32, (16, LANES), 0)
+    for j in range(CIN // 2):
+        part = jnp.broadcast_to(
+            wo_ref[0:1, LANES * j : LANES * j + LANES].astype(F32), (16, LANES)
+        )
+        wo32 = jnp.where(sub16 == 2 * j, part, wo32)
+        wo32 = jnp.where(sub16 == 2 * j + 1, roll(part, CH), wo32)
+    wo = wo32[:, 0:CH].astype(BF)
+    wot = wo32.T[0:CH].astype(BF)
+    zero64 = jnp.zeros((BS, BS), F32)
+    one = interp_ref[...].astype(F32)
+    matrix = jnp.concatenate(
+        [jnp.concatenate([one, zero64], axis=1), jnp.concatenate([zero64, one], axis=1)], axis=0
+    ).astype(BF)
+    cot3 = cot_ref[...].astype(F32)
+    cot = jnp.concatenate([cot3[:, q, :] for q in range(4)], axis=1).astype(BF)
+    wanted = tgt_ref[...] & 511
+    halves = jnp.concatenate([wanted >> 6, wanted & 63], axis=1).astype(F32).astype(BF)
+    own_row = lax.broadcasted_iota(jnp.int32, (rows, nt), 0)
+    own_peer = lax.broadcasted_iota(jnp.int32, (rows, nt), 1)
+    copies = jnp.where((own_row // KC) % nt == own_peer, 1.0, 0.0).astype(BF)
+    spots = jnp.dot(copies, halves, preferred_element_type=F32)
+    first_slot = lax.broadcasted_iota(jnp.int32, (rows, 1), 0) < nt * KC
+    target = jnp.where(
+        first_slot, spots[:, 0:1] * 64.0 + spots[:, 2:3], spots[:, 1:2] * 64.0 + spots[:, 3:4]
+    ).astype(jnp.int32)
 
     def ex_copy(e, d, arrival):
         ok, device = neighbour(d)
@@ -327,7 +480,6 @@
             table_ref[...], field, (((1,), (1,)), ((), ())), preferred_element_type=F32
         ).astype(BF)
 
-    sub16 = lax.broadcasted_iota(jnp.int32, (16, LANES), 0)
     takes = {
         2: (sub16 >= 1) & (sub16 <= 4),
         3: (sub16 >= 9) & (sub16 <= 12),
@@ -368,9 +520,15 @@
                 a * total + offset : a * total + offset + chans, count * LANES :
             ] = place(columns, table_ref, a)
 
+    groups = (
+        (na, send_a, recv_a, part_a, zrecv_a, done_a, all_a, 0),
+        (nb, send_b, recv_b, part_b, zrecv_b, done_b, all_b, 2),
+        (nc, send_c, recv_c, part_c, zrecv_c, done_c, all_c, 0),
+    )
+
     def xy_copy(g, k, arrival):
         other, device = xy_peer(k)
-        send, recv, m = ((send_a, recv_a, 16 * na), (send_b, recv_b, 16 * nb))[g]
+        send, recv, m = groups[g][1], groups[g][2], 16 * groups[g][0]
         at = other if arrival else me_xy
         return pltpu.make_async_remote_copy(
             src_ref=send.at[pl.ds(pl.multiple_of(other * m, 16), m)],
@@ -380,11 +538,6 @@
             device_id=device,
             device_id_type=MESH,
         )
-
-    groups = (
-        (na, send_a, recv_a, part_a, zrecv_a, done_a, all_a, 0),
-        (nb, send_b, recv_b, part_b, zrecv_b, done_b, all_b, 2),
-    )
 
     def xy_start(g):
         each(1, nxy, lambda k: xy_copy(g, k, False).start())
@@ -430,6 +583,26 @@
             device_id_type=MESH,
         )
 
+    def zall_copy(k, arrival):
+        other, device = z_peer(k)
+        return pltpu.make_async_remote_copy(
+            src_ref=part_c,
+            dst_ref=zrecv_c.at[other if arrival else z],
+            send_sem=za_ssem.at[k],
+            recv_sem=za_rsem.at[other if arrival else z],
+            device_id=device,
+            device_id_type=MESH,
+        )
+
+    def stage_all_z():
+        each(1, nz, lambda k: zall_copy(k, True).wait_recv())
+        zrecv_c[z] = part_c[...]
+        total = zrecv_c[0].astype(F32)
+        for j in range(1, nz):
+            total = total + zrecv_c[j].astype(F32)
+        done_c[...] = total.astype(BF)
+        each(1, nxy, lambda k: gx_copy(2, k, False).start())
+
     def stage_xy_to_z(g):
         n, send, recv, part, zrecv, done, full, first = groups[g]
         m = 16 * n
@@ -439,6 +612,9 @@
         for j in range(nxy):
             total = total + recv[j].astype(F32)
         part[...] = total.astype(BF)
+        if g == 2:
+            each(1, nz, lambda k: zall_copy(k, False).start())
+            return
         for q in range(n):
 
             @pl.when(z != z_owner(g, q))
@@ -477,6 +653,10 @@
         scale = 1.0 / math.sqrt(nf * 4 * nt * LANES)
         out_ref[...] = full[...].astype(F32) * scale
         each(1, nxy, lambda k: xy_copy(g, k, False).wait_send())
+        each(1, nxy, lambda k: gx_copy(g, k, False).wait_send())
+        if g == 2:
+            each(1, nz, lambda k: zall_copy(k, False).wait_send())
+            return
         for q in range(n):
 
             @pl.when(z != z_owner(g, q))
@@ -487,14 +667,12 @@
             def _(q=q):
                 each(1, nz, lambda k: zg_copy(g, q, k).wait_send())
 
-        each(1, nxy, lambda k: gx_copy(g, k, False).wait_send())
-
-    target = jnp.broadcast_to(tgt_ref[...], (rows, LANES))
+    target = jnp.broadcast_to(target, (rows, LANES))
     shift_in = target & (LANES - 1)
     to_tile = (target >> 7) + (lane < shift_in).astype(jnp.int32)
     each(0, nt, lambda k: box_arrival(k).wait_recv())
     arrived = jnp.concatenate([inbox[p] for p in range(nt)], axis=0)
-    moved = jnp.dot(arrived.astype(BF), interp_ref[...], preferred_element_type=F32)
+    moved = jnp.dot(arrived.astype(BF), matrix, preferred_element_type=F32)
     lane_half = lanes_of(rows // 2)
     moved = jnp.concatenate(
         [
@@ -516,7 +694,7 @@
             [jnp.where(sub8 < KC, total, 0.0), jnp.zeros((8, LANES), F32)], axis=0
         ).astype(BF)
         lifted.append(
-            jnp.concatenate([state_ref[:, q * LANES : (q + 1) * LANES], forcing], axis=0)
+            jnp.concatenate([state_rows[q].astype(BF), forcing], axis=0)
         )
 
     row_send[0, 0, 0:32] = lifted[0]
@@ -529,7 +707,7 @@
     fill_halo(
         x1, 32, 0, 32, 4, row_recv[0, 0, 0:32], row_recv[0, 1, 0:32], columns, placef_ref
     )
-    pre = conv_rows(a1_ref[...], x1, CH, 4, 1)
+    pre = conv_rows(a1[...], x1, CH, 4, 1)
     hidden_one, slope_one = [], []
     for r in range(4):
         value, slope = gelu_pair(pre[r])
@@ -568,7 +746,7 @@
         columns[CH : 2 * CH],
         placec_ref,
     )
-    pre = conv_rows(a2_ref[...], x2, 2 * CH, 2, 2)
+    pre = conv_rows(a2[...], x2, 2 * CH, 2, 2)
     hidden_two, slope_two = [], []
     for r in range(2):
         value, slope = gelu_pair(pre[r])
@@ -583,13 +761,13 @@
         x3, CH, 0, 3 * CH, 4, row_recv[1, 0, 0:CH], row_recv[1, 1, 0:CH], columns[0:CH], placef_ref
     )
     fill_centre(x3, 2 * CH, CH, 3 * CH, [hidden_two[r // 2] for r in range(4)])
-    back_three = jnp.dot(wot_ref[...], cot_ref[...], preferred_element_type=F32)
+    back_three = jnp.dot(wot, cot, preferred_element_type=F32)
     ex_wait(2)
     columns = halo_columns(2)
     fill_halo(
         x3, 2 * CH, CH, 3 * CH, 4, row_recv[2, 0], row_recv[2, 1], columns, placef_ref
     )
-    pre = conv_rows(a3_ref[...], x3, CH, 4, 1)
+    pre = conv_rows(a3[...], x3, CH, 4, 1)
     hidden_three, delta_three = [], []
     for r in range(4):
         value, slope = gelu_pair(pre[r])
@@ -605,11 +783,11 @@
     fill_centre(xd3, CH, 0, CH, delta_three)
     flat_three = jnp.concatenate(hidden_three, axis=1)
     pred_ref[...] = (
-        state_ref[...].astype(F32)
-        + jnp.dot(wo_ref[...], flat_three, preferred_element_type=F32)
+        jnp.concatenate(state_rows, axis=1)
+        + jnp.dot(wo, flat_three, preferred_element_type=F32)
     ).astype(BF)
     grad_out = lax.dot_general(
-        cot_ref[...], flat_three, (((1,), (1,)), ((), ())), preferred_element_type=F32
+        cot, flat_three, (((1,), (1,)), ((), ())), preferred_element_type=F32
     )
     grad_up = weight_grad([d.astype(F32) for d in delta_three], x3, 1)
     for block in range(4):
@@ -626,7 +804,7 @@
     fill_halo(
         xd3, CH, 0, CH, 4, row_recv[3, 0, 0:CH], row_recv[3, 1, 0:CH], columns, placef_ref
     )
-    join = conv_rows(b3_ref[...], xd3, 3 * CH, 4, 1)
+    join = conv_rows(b3[...], xd3, 3 * CH, 4, 1)
     delta_two = [
         (pair_sum(join[2 * r][CH:] + join[2 * r + 1][CH:]) * slope_two[r]).astype(BF)
         for r in range(2)
@@ -640,28 +818,34 @@
     grad_down = weight_grad([d.astype(F32) for d in delta_two], x2, 2)
     send_b[0:384] = grad_down[:, 0:LANES].astype(BF)
     send_b[384:576] = jnp.concatenate([grad_down[0:192, 128:192], grad_down[192:384, 128:192]], axis=1).astype(BF)
+    if 16 * nb * nxy > 576:
+        send_b[576:] = jnp.zeros((16 * nb * nxy - 576, LANES), BF)
+    xy_start(1)
+    stage_xy_to_z(0)
     ex_wait(4)
     columns = halo_columns(4)
     fill_halo(
         xd2, 2 * CH, 0, 2 * CH, 2, row_recv[4, 0], row_recv[4, 1], columns, placec_ref
     )
-    d_pool = conv_rows(b2_ref[...], xd2, CH, 2, 2)
+    d_pool = conv_rows(b2[...], xd2, CH, 2, 2)
     delta_one = [
         ((join[r][0:CH] + 0.25 * d_pool[r // 2]) * slope_one[r]).astype(BF).astype(F32)
         for r in range(4)
     ]
     grad_first = weight_grad(delta_one, x1, 1)
-    send_b[576:768] = jnp.concatenate([grad_first, jnp.zeros((192, 32), F32)], axis=1).astype(BF)
-    if 16 * nb * nxy > 768:
-        send_b[768:] = jnp.zeros((16 * nb * nxy - 768, LANES), BF)
-    xy_start(1)
-    stage_xy_to_z(0)
+    send_c[0:192] = jnp.concatenate([grad_first, jnp.zeros((192, 32), F32)], axis=1).astype(BF)
+    if 16 * nc * nxy > 192:
+        send_c[192:] = jnp.zeros((16 * nc * nxy - 192, LANES), BF)
+    xy_start(2)
     stage_xy_to_z(1)
     stage_z_reduce(0)
+    stage_xy_to_z(2)
     stage_z_reduce(1)
     stage_z_to_xy(0)
+    stage_all_z()
     stage_z_to_xy(1)
     stage_finish(0, ga_ref)
+    stage_finish(2, gc_ref)
     stage_finish(1, gb_ref)
     each(0, nt, lambda k: box_copy(k).wait_send())
 
@@ -682,49 +866,34 @@
     w_out,
 ):
     nxy, nz = nf * 2, nt // 2
-    na, nb = -(-55 // nxy), -(-48 // nxy)
+    na, nb, nc = -(-55 // nxy), -(-36 // nxy), -(-12 // nxy)
     nblk = source_start.shape[-1]
-    flat_state = state.reshape(CIN, 4 * LANES)
-    flat_cot = cotangent.reshape(CIN, 4 * LANES)
-    peer = block_peer.reshape(nblk)
-    target = jnp.repeat(target_start.reshape(nt, 2).T.reshape(2 * nt), KC)[:, None]
-    zero = jnp.zeros((BS, BS), BF)
-    matrix = interp[0]
-    pair = jnp.concatenate(
-        [jnp.concatenate([matrix, zero], 1), jnp.concatenate([zero, matrix], 1)], 0
-    )
-    first = jnp.pad(
-        w_first.reshape(3, 3, CH, CIN + KC), ((0, 0), (0, 0), (0, 0), (0, 12))
-    )
-    down = w_down.reshape(3, 3, 2 * CH, CH)
-    up = w_up.reshape(3, 3, CH, 3 * CH)
-    a1 = first.transpose(1, 2, 0, 3).reshape(3 * CH, 96)
-    a2 = down.transpose(1, 2, 0, 3).reshape(6 * CH, 3 * CH)
-    a3 = up.transpose(1, 2, 0, 3).reshape(3 * CH, 9 * CH)
-    b2 = down[::-1, ::-1].transpose(1, 3, 0, 2).reshape(3 * CH, 6 * CH)
-    b3 = up[::-1, ::-1].transpose(1, 3, 0, 2).reshape(9 * CH, 3 * CH)
-    wo = w_out.reshape(CIN, CH)
-    tables = [jnp.asarray(table, BF) for table in edge_tables()]
+    tables = [jnp.asarray(table, BF) for table in weight_tables() + edge_tables()]
     operands = (
-        flat_state,
-        flat_cot,
-        peer[None, :],
-        peer[:, None],
+        state[0],
+        cotangent[0],
+        block_peer.reshape(nblk, 1),
         source_start.reshape(1, nblk),
-        target,
-        pair,
-        sea_mask.reshape(4, LANES),
-        a1,
-        a2,
-        a3,
-        b2,
-        b3,
-        wo,
-        wo.T,
+        target_start.reshape(nt, 2),
+        interp[0],
+        sea_mask[0],
+        w_first[0],
+        w_down[0],
+        w_up[0],
+        w_out,
         *tables,
     )
     dma = pltpu.SemaphoreType.DMA
-    scratch = [
+    scratch = [pltpu.VMEM(op.shape, op.dtype) for op in operands]
+    scratch += [
+        dma((len(operands),)),
+        pltpu.VMEM((576, LANES), F32),
+        pltpu.VMEM((288, 384), F32),
+        pltpu.VMEM((3 * CH, 96), BF),
+        pltpu.VMEM((6 * CH, 3 * CH), BF),
+        pltpu.VMEM((3 * CH, 9 * CH), BF),
+        pltpu.VMEM((3 * CH, 6 * CH), BF),
+        pltpu.VMEM((9 * CH, 3 * CH), BF),
         pltpu.VMEM((nt, KC, LANES), F32),
         pltpu.VMEM((nt, KC, LANES), F32),
         pltpu.VMEM((N_EX, 2, LANES, LANES), BF),
@@ -737,12 +906,12 @@
         pltpu.VMEM((3 * CH, 5 * LANES), BF),
         pltpu.VMEM((6 * CH, 3 * LANES), BF),
     ]
-    for n in (na, nb):
+    for n in (na, nb, nc):
         scratch += [
             pltpu.VMEM((nxy * n * 16, LANES), BF),
             pltpu.VMEM((nxy, n * 16, LANES), BF),
             pltpu.VMEM((n * 16, LANES), BF),
-            pltpu.VMEM((n, nz, 16, LANES), BF),
+            pltpu.VMEM((nz, n * 16, LANES) if n == nc else (n, nz, 16, LANES), BF),
             pltpu.VMEM((n * 16, LANES), BF),
             pltpu.VMEM((nxy * n * 16, LANES), BF),
         ]
@@ -751,25 +920,28 @@
         dma((nt,)),
         dma((N_EX, 8)),
         dma((N_EX, 8)),
-        dma((2, nxy)),
-        dma((2, nxy)),
+        dma((3, nxy)),
+        dma((3, nxy)),
         dma((na + nb,)),
         dma((na + nb, nz)),
         dma((na + nb, nz)),
         dma((na + nb,)),
-        dma((2, nxy)),
-        dma((2, nxy)),
+        dma((3, nxy)),
+        dma((3, nxy)),
+        dma((nz,)),
+        dma((nz,)),
     ]
     vmem = pl.BlockSpec(memory_space=pltpu.VMEM)
-    predicted, sums_a, sums_b = pl.pallas_call(
-        functools.partial(kernel, nf, nt, na, nb),
+    predicted, sums_a, sums_b, sums_c = pl.pallas_call(
+        functools.partial(kernel, nf, nt, na, nb, nc),
         out_shape=(
             jax.ShapeDtypeStruct((CIN, 4 * LANES), BF),
             jax.ShapeDtypeStruct((nxy * na * 16, LANES), F32),
             jax.ShapeDtypeStruct((nxy * nb * 16, LANES), F32),
+            jax.ShapeDtypeStruct((nxy * nc * 16, LANES), F32),
         ),
-        in_specs=[vmem] * len(operands),
-        out_specs=(vmem, vmem, vmem),
+        in_specs=[pl.BlockSpec(memory_space=pl.ANY)] * len(operands),
+        out_specs=(vmem,) * 4,
         scratch_shapes=scratch,
         compiler_params=pltpu.CompilerParams(
             collective_id=0, has_side_effects=True, vmem_limit_bytes=40 * 2**20
@@ -785,7 +957,7 @@
         [sums_b[0:384], jnp.concatenate([sums_b[384:576, 0:64], sums_b[384:576, 64:128]], 0)],
         axis=1,
     )
-    grad_first = sums_b[576:768, 0:96].reshape(3, CH, 3, 32)[..., : CIN + KC]
+    grad_first = sums_c[0:192, 0:96].reshape(3, CH, 3, 32)[..., : CIN + KC]
     return (
         predicted.reshape(1, CIN, 4, LANES),
         grad_first.transpose(2, 0, 1, 3).reshape(1, 9, -1),

time: 99.5 us -> 104 us (1.045)
  the two profiles are of different devices: /device:TPU:4 before, /device:TPU:32 now
where the time goes in v2:
time: 104 us; the launch traced here: 103 us
  Pallas kernels  80.4 us (77%)
  local copies, waits for them, and re-layouts  21.6 us (21%)
    pallas_call x1, Pallas kernels, local(): pl.pallas_call(functools.partial(kernel, nf, nt, na, nb, nc), out_shape=(...  80.4 us
    unnamed x38, local copies, waits for them, and re-layouts  14 us

profile of v2, /device:TPU:32, one launch (start us, length us, event | category | flops | bytes accessed | tf_op | source)
XLA Modules:
  0.0 102.9 jit_solution(4963667464524135411)
XLA Ops:
  0.6 0.7 copy.37.peer_hbm
  1.4 0.8 copy.38.tgt_hbm
  2.1 0.0 copy-start
  2.1 1.4 %copy-done = bf16[1152,576]{1,0:T(8,128)(2,1)S(1)} copy-done((bf16[1152,576]{1,0:T(8,128)(2,1)S(1)}, bf16[1152,576]{1,0:T(8,128)(2,1)}, u32[]{:S(2)}) %copy-start) | copy-done | bytes 1327128
  3.5 0.0 copy-start.1
  3.5 1.0 copy-done.1
  4.5 0.0 copy-start.2
  4.5 1.0 copy-done.2
  5.5 0.0 copy-start.3
  5.5 1.0 copy-done.3
  6.5 0.0 copy-start.4
  6.5 0.9 copy-done.4
  7.4 0.0 copy-start.5
  7.4 0.9 copy-done.5
  8.4 0.0 copy-start.6
  8.4 0.8 copy-done.6
  9.1 0.0 copy-start.7
  9.1 0.7 copy-done.7
  9.8 0.0 copy-start.8
  9.8 0.7 copy-done.8
  10.6 0.0 copy-start.9
  10.6 0.7 copy-done.9
  11.3 0.0 copy-start.10
  11.3 0.7 copy-done.10
  12.0 0.0 copy-start.11
  12.0 0.7 copy-done.11
  12.7 0.0 copy-start.12
  12.7 0.7 copy-done.12
  13.4 0.0 copy-start.13
  13.4 0.7 copy-done.13
  14.1 0.0 copy-start.14
  14.1 0.7 copy-done.14
  14.8 0.0 copy-start.15
  14.8 0.7 copy-done.15
  15.5 0.0 copy-start.16
  15.5 0.7 copy-done.16
  16.1 80.4 %shard_map.218 = (bf16[16,512]{1,0:T(8,128)(2,1)S(1)}, f32[1024,128]{1,0:T(8,128)S(1)}, f32[768,128]{1,0:T(8,128)S(1)}, f32[256,128]{1,0:T(8,128)S(1)}) custom-call(bf16[16,4,128]{2,1,0:T(4,128)(2,1)S(1)} %bitcast.27, bf16[16,4,128]{2,1,0:T(4,128)(2,1)S(1)} %bitcast.28, s32[32,1]{1,0:T(8,128)S(1)} %copy.37.peer_hbm, s32[1,32]{1,0:T(1,128)S(1)} %bitcast.31, ...), custom_call_target="tpu_custom_call" | custom-call | tf_op jit(solution)/shard_map/pallas_call | solution.py:935
  96.6 0.6 reshape.46
  97.2 0.7 reshape.53
  97.9 0.1 copy.39
  98.0 0.1 reshape.47
  98.1 0.1 fusion
  98.2 0.2 copy.40
  98.4 0.9 reshape.54
  99.3 0.1 fusion.1
  99.4 0.1 copy.41
  99.6 0.1 reshape.49
  99.7 0.2 copy.42
  99.9 1.1 %reshape.55 = f32[1,9,8192]{2,0,1:T(1,128)} reshape(f32[3,3,128,64]{3,2,1,0:T(8,128)S(1)} %copy.42) | data formatting | bytes 589824 | tf_op jit(solution)/shard_map/reshape | solution.py:964
  101.1 0.3 reshape.51
  101.4 0.1 copy.43
  101.5 1.3 %reshape.56 = f32[1,9,12288]{2,0,1:T(1,128)} reshape(f32[3,3,64,192]{3,2,1,0:T(8,128)S(1)} %copy.43) | data formatting | bytes 884736 | tf_op jit(solution)/shard_map/reshape | solution.py:965
  (10 shorter events, 0.1 us)
Async XLA Ops:
  2.1 1.4 %copy-start = (bf16[1152,576]{1,0:T(8,128)(2,1)S(1)}, bf16[1152,576]{1,0:T(8,128)(2,1)}, u32[]{:S(2)}) copy-start(bf16[1152,576]{1,0:T(8,128)(2,1)} %constant.17.clone.down_hbm) | copy-start | bytes 3981316
  3.5 1.0 copy-start.1
  4.5 1.0 copy-start.2
  5.5 1.0 copy-start.3
  6.5 0.9 copy-start.4
  7.4 0.9 copy-start.5
  8.4 0.8 copy-start.6
  9.1 0.7 copy-start.7
  9.8 0.7 copy-start.8
  10.6 0.7 copy-start.9
  11.3 0.7 copy-start.10
  12.0 0.7 copy-start.11
  12.7 0.7 copy-start.12
  13.4 0.7 copy-start.13
  14.1 0.7 copy-start.14
  14.8 0.7 copy-start.15
  15.5 0.7 copy-start.16

commit v3 on v2

--- a/solution.py
+++ b/solution.py
@@ -55,12 +55,6 @@
 
 
 def edge_tables():
-    pick_fine = np.zeros((16, 4 * LANES), np.float32)
-    pick_coarse = np.zeros((16, 2 * LANES), np.float32)
-    for base, lane in ((0, LANES - 1), (8, 0)):
-        for j, row in enumerate((3, 0, 1, 2, 3, 0)):
-            pick_fine[base + j, row * LANES + lane] = 1
-            pick_coarse[base + j, (row // 2) * LANES + lane] = 1
     place_fine = np.zeros((3, 16, LANES), np.float32)
     place_coarse = np.zeros((3, 16, LANES), np.float32)
     for a in range(3):
@@ -69,24 +63,19 @@
                 place_fine[a, base + r + a, start + r] = 1
             for r in range(2):
                 place_coarse[a, base + (0, 1, 3, 5)[r + a], start + r] = 1
-    return pick_fine, pick_coarse, place_fine, place_coarse
-
-
-def weight_tables():
-    up = np.zeros((576, 288), np.float32)
-    down = np.zeros((1152, 576), np.float32)
-    for b in range(3):
-        for a in range(3):
-            k = 3 * (2 - a) + 2 - b
-            for o in range(CH):
-                up[(b * 3 + a) * CH + o, 8 * (o // 2) + k if k < 8 else 256 + o // 2] = 1
-            for o in range(2 * CH):
-                down[(b * 3 + a) * 2 * CH + o, 8 * (o // 2) + k if k < 8 else 512 + o // 2] = 1
+    return place_fine, place_coarse
+
+
+def first_tables():
     wide = CIN + KC
-    lane = np.arange(CH * wide)
-    mask = (lane[None, :] // wide == np.arange(CH)[:, None]).astype(np.float32)
-    fold = (lane[:, None] % wide == np.arange(32)[None, :]).astype(np.float32)
-    return up, down, mask, fold
+    tables = np.zeros((2, 9 * CH, LANES), np.float32)
+    for k in range(9):
+        for o in range(CH):
+            for step in range(2):
+                t = o * wide // LANES + step
+                if t < CH * wide // LANES:
+                    tables[step, k * CH + o, 8 * t + k if k < 8 else 80 + t] = 1
+    return (tables,)
 
 
 def conv_rows(weight, x_ref, outs, rows, step):
@@ -144,18 +133,14 @@
     w2_hbm,
     w3_hbm,
     wo_hbm,
-    up_hbm,
-    down_hbm,
-    mask_hbm,
-    fold_hbm,
-    pickf_hbm,
-    pickc_hbm,
+    find_hbm,
     placef_hbm,
     placec_hbm,
     pred_ref,
-    ga_ref,
-    gb_ref,
-    gc_ref,
+    gfirst_ref,
+    gdown_ref,
+    gup_ref,
+    gout_ref,
     state_ref,
     cot_ref,
     peer_ref,
@@ -167,17 +152,16 @@
     w2_ref,
     w3_ref,
     wo_ref,
-    up_ref,
-    down_ref,
-    mask_ref,
-    fold_ref,
-    pickf_ref,
-    pickc_ref,
+    find_ref,
     placef_ref,
     placec_ref,
     load_sem,
+    s1,
     s2,
     s3,
+    u2,
+    u3,
+    pred32,
     a1,
     a2,
     a3,
@@ -261,19 +245,14 @@
                 (peer_hbm, peer_ref),
                 (src_hbm, src_ref),
                 (w3_hbm, w3_ref),
-                (up_hbm, up_ref),
                 (w2_hbm, w2_ref),
-                (down_hbm, down_ref),
                 (w1_hbm, w1_ref),
-                (mask_hbm, mask_ref),
-                (fold_hbm, fold_ref),
+                (find_hbm, find_ref),
                 (wo_hbm, wo_ref),
                 (tgt_hbm, tgt_ref),
                 (interp_hbm, interp_ref),
                 (sea_hbm, sea_ref),
                 (cot_hbm, cot_ref),
-                (pickf_hbm, pickf_ref),
-                (pickc_hbm, pickc_ref),
                 (placef_hbm, placef_ref),
                 (placec_hbm, placec_ref),
             )
@@ -313,11 +292,14 @@
         load.wait()
     state3 = state_ref[...].astype(F32)
     state_rows = [state3[:, q, :] for q in range(4)]
-    peer_col = jnp.broadcast_to(peer_ref[...], (nblk, nblk))
+    peer_row = jnp.broadcast_to(peer_ref[...], (nblk, nblk))
     diagonal = lax.broadcasted_iota(jnp.int32, (nblk, nblk), 0) == lax.broadcasted_iota(
         jnp.int32, (nblk, nblk), 1
     )
-    peer_row = jnp.sum(jnp.where(diagonal, peer_col, 0), axis=0, keepdims=True)
+    peer_col = jnp.sum(
+        jnp.where(diagonal, peer_row, 0).astype(F32), axis=1, keepdims=True
+    ).astype(jnp.int32)
+    peer_row = peer_row[0:1]
     same = peer_col == peer_row
     earlier = lax.broadcasted_iota(jnp.int32, (nblk, nblk), 0) < lax.broadcasted_iota(
         jnp.int32, (nblk, nblk), 1
@@ -348,6 +330,32 @@
     for p in range(nt):
         outbox[p] = packed[p * KC : (p + 1) * KC]
 
+    loads[3].wait()
+    for j in range(CH // 2):
+        for t in range(3):
+            at = 384 * j + 128 * t
+            part = w3_ref[:, at : at + 128].astype(F32)
+            s3[t, 8 * j : 8 * j + 8] = part[0:8]
+            s3[t, 256 + j : 257 + j] = part[8:9]
+    lane_j = lanes_of(CH // 2)
+    for b in range(3):
+        for a in range(3):
+            k = 3 * a + b
+            parts = [
+                s3[t, pl.ds(k, CH // 2, stride=8), :] if k < 8 else s3[t, 256:288]
+                for t in range(3)
+            ]
+            last = roll(parts[2], CH)
+            u3[k, 0, pl.ds(0, CH // 2, stride=2), :] = parts[0]
+            u3[k, 1, pl.ds(0, CH // 2, stride=2), :] = parts[1]
+            u3[k, 0, pl.ds(1, CH // 2, stride=2), :] = jnp.where(
+                lane_j < CH, roll(parts[1], CH), last
+            )
+            u3[k, 1, pl.ds(1, CH // 2, stride=2), :] = last
+            tap = jnp.concatenate([u3[k, 0], u3[k, 1][:, 0:CH]], axis=1)
+            a3[CH * b : CH * b + CH, 192 * a : 192 * a + 192] = tap.astype(BF)
+            b3[192 * (2 - b) : 192 * (3 - b), CH * (2 - a) : CH * (3 - a)] = tap.T.astype(BF)
+
     pl.semaphore_wait(barrier, expected)
 
     def box_copy(k):
@@ -381,40 +389,45 @@
 
     each(0, nt, lambda k: box_copy(k).start())
 
-    for load in loads[3:]:
+    for load in loads[4:]:
         load.wait()
-    for j in range(CH // 2):
-        part = w3_ref[:, 384 * j : 384 * j + 384].astype(F32)
-        s3[8 * j : 8 * j + 8] = part[0:8]
-        s3[256 + j : 257 + j] = part[8:9]
     for j in range(CH):
         part = w2_ref[:, 128 * j : 128 * j + 128].astype(F32)
         s2[8 * j : 8 * j + 8] = part[0:8]
         s2[512 + j : 513 + j] = part[8:9]
-    taps = jnp.dot(up_ref[...], s3[...].astype(BF), preferred_element_type=F32)
-    odd = (lax.broadcasted_iota(jnp.int32, (576, 192), 0) & 1) == 1
-    taps = jnp.where(odd, taps[:, 192:384], taps[:, 0:192])
     for b in range(3):
-        b3[192 * b : 192 * b + 192] = taps[192 * b : 192 * b + 192].T.astype(BF)
         for a in range(3):
-            at = ((2 - b) * 3 + 2 - a) * CH
-            a3[CH * b : CH * b + CH, 192 * a : 192 * a + 192] = taps[at : at + CH].astype(BF)
-    taps = jnp.dot(down_ref[...], s2[...].astype(BF), preferred_element_type=F32)
-    odd = (lax.broadcasted_iota(jnp.int32, (1152, LANES), 0) & 1) == 1
-    taps = jnp.where(odd, roll(taps, CH), taps)
+            k = 3 * a + b
+            part = s2[pl.ds(k, CH, stride=8), :] if k < 8 else s2[512:576]
+            u2[k, pl.ds(0, CH, stride=2), :] = part
+            u2[k, pl.ds(1, CH, stride=2), :] = roll(part, CH)
+            tap = u2[k]
+            a2[2 * CH * b : 2 * CH * b + 2 * CH, CH * a : CH * a + CH] = tap[
+                :, 0:CH
+            ].astype(BF)
+            b2[CH * (2 - b) : CH * (3 - b), 2 * CH * (2 - a) : 2 * CH * (3 - a)] = tap.T[
+                0:CH
+            ].astype(BF)
+    s1[...] = jnp.zeros_like(s1)
+    for j in range(10):
+        part = w1_ref[:, 128 * j : 128 * j + 128].astype(F32)
+        s1[8 * j : 8 * j + 8] = part[0:8]
+        s1[80 + j : 81 + j] = part[8:9]
+    flat_first = s1[...].astype(BF)
+    begins = jnp.dot(find_ref[0], flat_first, preferred_element_type=F32)
+    follows = jnp.dot(find_ref[1], flat_first, preferred_element_type=F32)
+    lane_first = lanes_of(9 * CH)
+    offset = (
+        (lax.broadcasted_iota(jnp.int32, (9 * CH, LANES), 0) % CH) * (CIN + KC)
+    ) & (LANES - 1)
+    taps = barrel(jnp.where(lane_first >= offset, begins, follows), offset, False)
+    taps = jnp.where(lane_first < CIN + KC, taps, 0.0)
     for b in range(3):
-        b2[CH * b : CH * b + CH] = taps[384 * b : 384 * b + 384].T[0:CH].astype(BF)
         for a in range(3):
-            at = ((2 - b) * 3 + 2 - a) * 2 * CH
-            a2[2 * CH * b : 2 * CH * b + 2 * CH, CH * a : CH * a + CH] = taps[
-                at : at + 2 * CH, 0:CH
+            k = 3 * a + b
+            a1[CH * b : CH * b + CH, 32 * a : 32 * a + 32] = taps[
+                CH * k : CH * k + CH, 0:32
             ].astype(BF)
-    flat_first = w1_ref[...].astype(F32)
-    for k in range(9):
-        spread = mask_ref[...].astype(F32) * flat_first[k : k + 1]
-        a1[CH * (k % 3) : CH * (k % 3) + CH, 32 * (k // 3) : 32 * (k // 3) + 32] = jnp.dot(
-            spread.astype(BF), fold_ref[...], preferred_element_type=F32
-        ).astype(BF)
     wo32 = jnp.zeros((16, LANES), F32)
     sub16 = lax.broadcasted_iota(jnp.int32, (16, LANES), 0)
     for j in range(CIN // 2):
@@ -433,11 +446,13 @@
     cot3 = cot_ref[...].astype(F32)
     cot = jnp.concatenate([cot3[:, q, :] for q in range(4)], axis=1).astype(BF)
     wanted = tgt_ref[...] & 511
-    halves = jnp.concatenate([wanted >> 6, wanted & 63], axis=1).astype(F32).astype(BF)
+    halves = jnp.concatenate([wanted >> 6, wanted & 63], axis=0).astype(F32).astype(BF)
     own_row = lax.broadcasted_iota(jnp.int32, (rows, nt), 0)
     own_peer = lax.broadcasted_iota(jnp.int32, (rows, nt), 1)
     copies = jnp.where((own_row // KC) % nt == own_peer, 1.0, 0.0).astype(BF)
-    spots = jnp.dot(copies, halves, preferred_element_type=F32)
+    spots = lax.dot_general(
+        copies, halves, (((1,), (1,)), ((), ())), preferred_element_type=F32
+    )
     first_slot = lax.broadcasted_iota(jnp.int32, (rows, 1), 0) < nt * KC
     target = jnp.where(
         first_slot, spots[:, 0:1] * 64.0 + spots[:, 2:3], spots[:, 1:2] * 64.0 + spots[:, 3:4]
@@ -475,9 +490,23 @@
                 copy.wait_recv()
                 copy.wait_send()
 
-    def pick(table_ref, field):
+    def edge_pick(rows_of):
+        parts = []
+        for targets in rows_of:
+            right, left = sub16 < 0, sub16 < 0
+            for j in targets:
+                right, left = right | (sub16 == j), left | (sub16 == j + 8)
+            hit = (right & (lane16 == LANES - 1)) | (left & (lane16 == 0))
+            parts.append(jnp.where(hit, 1.0, 0.0))
+        return jnp.concatenate(parts, axis=1).astype(BF)
+
+    lane16 = lanes_of(16)
+    pick_fine = edge_pick(((1, 5), (2,), (3,), (0, 4)))
+    pick_coarse = edge_pick(((1, 2, 5), (0, 3, 4)))
+
+    def pick(table, field):
         return lax.dot_general(
-            table_ref[...], field, (((1,), (1,)), ((), ())), preferred_element_type=F32
+            table, field, (((1,), (1,)), ((), ())), preferred_element_type=F32
         ).astype(BF)
 
     takes = {
@@ -645,13 +674,11 @@
 
         each(1, nxy, lambda k: gx_copy(g, k, False).start())
 
-    def stage_finish(g, out_ref):
+    def stage_finish(g):
         n, send, recv, part, zrecv, done, full, first = groups[g]
         m = 16 * n
         each(1, nxy, lambda k: gx_copy(g, k, True).wait_recv())
         full[pl.ds(pl.multiple_of(me_xy * m, 16), m), :] = done[...]
-        scale = 1.0 / math.sqrt(nf * 4 * nt * LANES)
-        out_ref[...] = full[...].astype(F32) * scale
         each(1, nxy, lambda k: xy_copy(g, k, False).wait_send())
         each(1, nxy, lambda k: gx_copy(g, k, False).wait_send())
         if g == 2:
@@ -699,7 +726,7 @@
 
     row_send[0, 0, 0:32] = lifted[0]
     row_send[0, 1, 0:32] = lifted[3]
-    edge_send[0, :, 0:32] = pick(pickf_ref, jnp.concatenate(lifted, axis=1))
+    edge_send[0, :, 0:32] = pick(pick_fine, jnp.concatenate(lifted, axis=1))
     ex_start(0)
     fill_centre(x1, 32, 0, 32, lifted)
     ex_wait(0)
@@ -725,8 +752,8 @@
         row_send[1, at, CH : 2 * CH] = pooled[coarse]
     edge_send[1] = jnp.concatenate(
         [
-            pick(pickf_ref, jnp.concatenate(hidden_one, axis=1)),
-            pick(pickc_ref, jnp.concatenate(pooled, axis=1)),
+            pick(pick_fine, jnp.concatenate(hidden_one, axis=1)),
+            pick(pick_coarse, jnp.concatenate(pooled, axis=1)),
         ],
         axis=1,
     )
@@ -755,7 +782,7 @@
 
     row_send[2, 0] = hidden_two[0]
     row_send[2, 1] = hidden_two[1]
-    edge_send[2] = pick(pickc_ref, jnp.concatenate(hidden_two, axis=1))
+    edge_send[2] = pick(pick_coarse, jnp.concatenate(hidden_two, axis=1))
     ex_start(2)
     fill_halo(
         x3, CH, 0, 3 * CH, 4, row_recv[1, 0, 0:CH], row_recv[1, 1, 0:CH], columns[0:CH], placef_ref
@@ -778,23 +805,43 @@
 
     row_send[3, 0, 0:CH] = delta_three[0]
     row_send[3, 1, 0:CH] = delta_three[3]
-    edge_send[3, :, 0:CH] = pick(pickf_ref, jnp.concatenate(delta_three, axis=1))
+    edge_send[3, :, 0:CH] = pick(pick_fine, jnp.concatenate(delta_three, axis=1))
     ex_start(3)
     fill_centre(xd3, CH, 0, CH, delta_three)
     flat_three = jnp.concatenate(hidden_three, axis=1)
-    pred_ref[...] = (
-        jnp.concatenate(state_rows, axis=1)
-        + jnp.dot(wo, flat_three, preferred_element_type=F32)
-    ).astype(BF)
+    change = jnp.dot(wo, flat_three, preferred_element_type=F32)
+    for r in range(4):
+        pred32[:, r, :] = state_rows[r] + change[:, r * LANES : (r + 1) * LANES]
+    pred_ref[...] = pred32[...].astype(BF)
     grad_out = lax.dot_general(
         cot, flat_three, (((1,), (1,)), ((), ())), preferred_element_type=F32
     )
     grad_up = weight_grad([d.astype(F32) for d in delta_three], x3, 1)
-    for block in range(4):
-        send_a[192 * block : 192 * block + 192] = grad_up[
-            :, block * LANES : (block + 1) * LANES
-        ].astype(BF)
-    send_a[768:864] = jnp.concatenate([grad_up[0:96, 512:576], grad_up[96:192, 512:576]], axis=1).astype(BF)
+    tiles = [grad_up[:, LANES * t : LANES * t + LANES] for t in range(4)]
+    tiles.append(jnp.concatenate([grad_up[:, 512:576], jnp.zeros((192, CH), F32)], axis=1))
+    lane_up = lanes_of(192)
+    second = roll(tiles[2], CH)
+    starts = (
+        (tiles[0], tiles[1]),
+        (jnp.where(lane_up < CH, roll(tiles[1], CH), second), second),
+        (tiles[3], tiles[4]),
+    )
+    for a in range(3):
+        for t in range(2):
+            u3[3 * a, t] = starts[a][t][0:CH]
+            u3[3 * a + 1, t] = starts[a][t][CH : 2 * CH]
+            u3[3 * a + 2, t] = starts[a][t][2 * CH : 3 * CH]
+    for k in range(9):
+        even = [u3[k, t, pl.ds(0, CH // 2, stride=2), :] for t in range(2)]
+        uneven = [roll(u3[k, t, pl.ds(1, CH // 2, stride=2), :], CH) for t in range(2)]
+        pairs = (
+            even[0],
+            jnp.where(lane_j < CH, even[1], uneven[0]),
+            jnp.where(lane_j < CH, uneven[0], uneven[1]),
+        )
+        for t in range(3):
+            at = 32 * (9 * t + k)
+            send_a[at : at + 32] = pairs[t].astype(BF)
     send_a[864:880] = jnp.concatenate([grad_out, jnp.zeros((16, 64), F32)], axis=1).astype(BF)
     if 16 * na * nxy > 880:
         send_a[880:] = jnp.zeros((16 * na * nxy - 880, LANES), BF)
@@ -812,12 +859,25 @@
 
     row_send[4, 0] = delta_two[0]
     row_send[4, 1] = delta_two[1]
-    edge_send[4] = pick(pickc_ref, jnp.concatenate(delta_two, axis=1))
+    edge_send[4] = pick(pick_coarse, jnp.concatenate(delta_two, axis=1))
     ex_start(4)
     fill_centre(xd2, 2 * CH, 0, 2 * CH, delta_two)
     grad_down = weight_grad([d.astype(F32) for d in delta_two], x2, 2)
-    send_b[0:384] = grad_down[:, 0:LANES].astype(BF)
-    send_b[384:576] = jnp.concatenate([grad_down[0:192, 128:192], grad_down[192:384, 128:192]], axis=1).astype(BF)
+    lane_down = lanes_of(CH)
+    right = jnp.concatenate([grad_down[:, 128:192], jnp.zeros((384, CH), F32)], axis=1)
+    for b in range(3):
+        u2[b] = grad_down[2 * CH * b : 2 * CH * b + 2 * CH, 0:LANES]
+        u2[3 + b] = right[2 * CH * b : 2 * CH * b + 2 * CH]
+    for b in range(3):
+        for a in range(3):
+            even = u2[3 * (a // 2) + b, pl.ds(0, CH, stride=2), :]
+            uneven = u2[3 * (a // 2) + b, pl.ds(1, CH, stride=2), :]
+            if a == 1:
+                pair = jnp.where(lane_down < CH, roll(even, CH), uneven)
+            else:
+                pair = jnp.where(lane_down < CH, even, roll(uneven, CH))
+            at = CH * (3 * a + b)
+            send_b[at : at + CH] = pair.astype(BF)
     if 16 * nb * nxy > 576:
         send_b[576:] = jnp.zeros((16 * nb * nxy - 576, LANES), BF)
     xy_start(1)
@@ -844,9 +904,61 @@
     stage_z_to_xy(0)
     stage_all_z()
     stage_z_to_xy(1)
-    stage_finish(0, ga_ref)
-    stage_finish(2, gc_ref)
-    stage_finish(1, gb_ref)
+    scale = 1.0 / math.sqrt(nf * 4 * nt * LANES)
+    stage_finish(0)
+    for t in range(3):
+        for k in range(9):
+            at = 32 * (9 * t + k)
+            part = all_a[at : at + 32].astype(F32) * scale
+            if k < 8:
+                s3[t, pl.ds(k, CH // 2, stride=8), :] = part
+            else:
+                s3[t, 256:288] = part
+    for j in range(CH // 2):
+        for t in range(3):
+            at = 384 * j + 128 * t
+            gup_ref[0:8, at : at + 128] = s3[t, 8 * j : 8 * j + 8]
+            gup_ref[8:9, at : at + 128] = s3[t, 256 + j : 257 + j]
+    part = all_a[864:880].astype(F32) * scale
+    turned = roll(part, CH)
+    lane1 = lanes_of(1)
+    for j in range(CIN // 2):
+        gout_ref[0:1, LANES * j : LANES * j + LANES] = jnp.where(
+            lane1 < CH, part[2 * j : 2 * j + 1], turned[2 * j + 1 : 2 * j + 2]
+        )
+    stage_finish(2)
+    sums = all_c[0:192].astype(F32)
+    taps = jnp.concatenate(
+        [
+            roll(sums[CH * b : CH * b + CH], -32 * a) if a else sums[CH * b : CH * b + CH]
+            for a in range(3)
+            for b in range(3)
+        ],
+        axis=0,
+    )
+    taps = barrel(jnp.where(lane_first < CIN + KC, taps, 0.0), offset, True)
+    flat_first = sum(
+        lax.dot_general(
+            find_ref[step],
+            jnp.where((lane_first >= offset) == (step == 0), taps, 0.0).astype(BF),
+            (((0,), (0,)), ((), ())),
+            preferred_element_type=F32,
+        )
+        for step in range(2)
+    )
+    for j in range(10):
+        gfirst_ref[0:8, 128 * j : 128 * j + 128] = flat_first[8 * j : 8 * j + 8] * scale
+        gfirst_ref[8:9, 128 * j : 128 * j + 128] = flat_first[80 + j : 81 + j] * scale
+    stage_finish(1)
+    for k in range(9):
+        part = all_b[CH * k : CH * k + CH].astype(F32) * scale
+        if k < 8:
+            s2[pl.ds(k, CH, stride=8), :] = part
+        else:
+            s2[512:576] = part
+    for j in range(CH):
+        gdown_ref[0:8, 128 * j : 128 * j + 128] = s2[8 * j : 8 * j + 8]
+        gdown_ref[8:9, 128 * j : 128 * j + 128] = s2[512 + j : 513 + j]
     each(0, nt, lambda k: box_copy(k).wait_send())
 
 
@@ -868,13 +980,13 @@
     nxy, nz = nf * 2, nt // 2
     na, nb, nc = -(-55 // nxy), -(-36 // nxy), -(-12 // nxy)
     nblk = source_start.shape[-1]
-    tables = [jnp.asarray(table, BF) for table in weight_tables() + edge_tables()]
+    tables = [jnp.asarray(table, BF) for table in first_tables() + edge_tables()]
     operands = (
         state[0],
         cotangent[0],
-        block_peer.reshape(nblk, 1),
+        block_peer.reshape(1, nblk),
         source_start.reshape(1, nblk),
-        target_start.reshape(nt, 2),
+        target_start.reshape(nt, 2).T,
         interp[0],
         sea_mask[0],
         w_first[0],
@@ -887,8 +999,12 @@
     scratch = [pltpu.VMEM(op.shape, op.dtype) for op in operands]
     scratch += [
         dma((len(operands),)),
+        pltpu.VMEM((LANES, LANES), F32),
         pltpu.VMEM((576, LANES), F32),
-        pltpu.VMEM((288, 384), F32),
+        pltpu.VMEM((3, 288, LANES), F32),
+        pltpu.VMEM((9, 2 * CH, LANES), F32),
+        pltpu.VMEM((9, 2, CH, LANES), F32),
+        pltpu.VMEM((CIN, 4, LANES), F32),
         pltpu.VMEM((3 * CH, 96), BF),
         pltpu.VMEM((6 * CH, 3 * CH), BF),
         pltpu.VMEM((3 * CH, 9 * CH), BF),
@@ -932,39 +1048,24 @@
         dma((nz,)),
     ]
     vmem = pl.BlockSpec(memory_space=pltpu.VMEM)
-    predicted, sums_a, sums_b, sums_c = pl.pallas_call(
+    predicted, grad_first, grad_down, grad_up, grad_out = pl.pallas_call(
         functools.partial(kernel, nf, nt, na, nb, nc),
         out_shape=(
-            jax.ShapeDtypeStruct((CIN, 4 * LANES), BF),
-            jax.ShapeDtypeStruct((nxy * na * 16, LANES), F32),
-            jax.ShapeDtypeStruct((nxy * nb * 16, LANES), F32),
-            jax.ShapeDtypeStruct((nxy * nc * 16, LANES), F32),
+            jax.ShapeDtypeStruct((CIN, 4, LANES), BF),
+            jax.ShapeDtypeStruct(w_first.shape[1:], F32),
+            jax.ShapeDtypeStruct(w_down.shape[1:], F32),
+            jax.ShapeDtypeStruct(w_up.shape[1:], F32),
+            jax.ShapeDtypeStruct(w_out.shape, F32),
         ),
-        in_specs=[pl.BlockSpec(memory_space=pl.ANY)] * len(operands),
-        out_specs=(vmem,) * 4,
+        in_specs=[pl.BlockSpec(memory_space=pltpu.HBM)] * len(operands),
+        out_specs=(vmem,) * 5,
         scratch_shapes=scratch,
         compiler_params=pltpu.CompilerParams(
-            collective_id=0, has_side_effects=True, vmem_limit_bytes=40 * 2**20
+            collective_id=0, has_side_effects=True, vmem_limit_bytes=64 * 2**20
         ),
     )(*operands)
 
-    grad_up = jnp.concatenate(
-        [sums_a[192 * i : 192 * i + 192] for i in range(4)]
-        + [jnp.concatenate([sums_a[768:864, 0:64], sums_a[768:864, 64:128]], 0)],
-        axis=1,
-    )
-    grad_down = jnp.concatenate(
-        [sums_b[0:384], jnp.concatenate([sums_b[384:576, 0:64], sums_b[384:576, 64:128]], 0)],
-        axis=1,
-    )
-    grad_first = sums_c[0:192, 0:96].reshape(3, CH, 3, 32)[..., : CIN + KC]
-    return (
-        predicted.reshape(1, CIN, 4, LANES),
-        grad_first.transpose(2, 0, 1, 3).reshape(1, 9, -1),
-        grad_down.reshape(3, 2 * CH, 3, CH).transpose(2, 0, 1, 3).reshape(1, 9, -1),
-        grad_up.reshape(3, CH, 3, 3 * CH).transpose(2, 0, 1, 3).reshape(1, 9, -1),
-        sums_a[864:880, 0:64].reshape(1, -1),
-    )
+    return predicted[None], grad_first[None], grad_down[None], grad_up[None], grad_out
 
 
 def solution(mesh):

time: 104 us -> 87.4 us (0.84)
  the two profiles are of different devices: /device:TPU:32 before, /device:TPU:8 now
where the time goes in v3:
time: 87.4 us; the launch traced here: 87.1 us
  Pallas kernels  80.3 us (92%)
  local copies, waits for them, and re-layouts  6.18 us (7%)
    pallas_call x1, Pallas kernels, local(): pl.pallas_call(functools.partial(kernel, nf, nt, na, nb, nc), out_shape=(...  80.3 us
    unnamed x11, local copies, waits for them, and re-layouts  6.18 us

profile of v3, /device:TPU:8, one launch (start us, length us, event | category | flops | bytes accessed | tf_op | source)
XLA Modules:
  0.0 87.1 jit_solution(144599603823481824)
XLA Ops:
  0.6 80.3 %shard_map.173 = (bf16[16,4,128]{2,1,0:T(4,128)(2,1)}, f32[9,1280]{1,0:T(8,128)}, f32[9,8192]{1,0:T(8,128)}, f32[9,12288]{1,0:T(8,128)}, f32[1,1024]{1,0:T(1,128)}) custom-call(bf16[16,4,128]{2,1,0:T(4,128)(2,1)} %bitcast.22, bf16[16,4,128]{2,1,0:T(4,128)(2,1)} %bitcast.23, s32[1,32]{1,0:T(1,128)} %bitcast.28, s32[1,32]{1,0:T(1,128)} %bitcast.29, ...), custom_call_target="tpu_custom_call" | custom-call | tf_op jit(solution)/shard_map/pallas_call | solution.py:1051
  80.9 0.0 copy-start
  81.0 1.6 %copy.19 = f32[1,9,1280]{2,0,1:T(1,128)} copy(f32[1,9,1280]{2,1,0:T(8,128)} %bitcast.20) | data formatting | bytes 92160
  82.6 2.1 %copy.20 = f32[1,9,8192]{2,0,1:T(1,128)} copy(f32[1,9,8192]{2,1,0:T(8,128)} %bitcast.17) | data formatting | bytes 589824
  84.6 0.0 copy-done
  84.6 0.0 copy-start.1
  84.6 1.2 %copy.21 = f32[1,9,12288]{2,0,1:T(1,128)} copy(f32[1,9,12288]{2,1,0:T(8,128)S(1)} %bitcast.16) | data formatting | bytes 884736
  85.9 0.0 copy-done.1
  85.9 0.0 copy-start.2
  85.9 0.6 copy.24
  86.5 0.1 copy-done.2
  86.5 0.6 copy.25
Async XLA Ops:
  80.9 3.7 %copy-start = (f32[9,12288]{1,0:T(8,128)S(1)}, f32[9,12288]{1,0:T(8,128)}, u32[]{:S(2)}) copy-start(f32[9,12288]{1,0:T(8,128)} %get-tuple-element.13) | copy-start | bytes 1327108
  84.6 1.2 %copy-start.1 = (bf16[16,4,128]{2,1,0:T(4,128)(2,1)S(1)}, bf16[16,4,128]{2,1,0:T(4,128)(2,1)}, u32[]{:S(2)}) copy-start(bf16[16,4,128]{2,1,0:T(4,128)(2,1)} %get-tuple-element.10) | copy-start | bytes 49156
  85.9 0.7 copy-start.2

commit v4 on v3

--- a/solution.py
+++ b/solution.py
@@ -20,8 +20,16 @@
 MESH = pl.DeviceIdType.MESH
 DIRS = [(-1, 0), (1, 0), (0, -1), (0, 1), (-1, -1), (-1, 1), (1, -1), (1, 1)]
 OPP = [DIRS.index((-a, -b)) for a, b in DIRS]
-N_EX = 5
-EX_CH = (32, 128, 128, 64, 128)
+WIDE_CH = (32, CH)
+PITCH = 6
+
+
+def fine_lanes(r):
+    return PITCH * (r + 3) + 2, 64 + PITCH * (r + 3) + 3
+
+
+def coarse_lanes(r):
+    return PITCH * (2 * r + 3) + 1, 64 + PITCH * (2 * r + 3) + 3
 
 
 def gelu_pair(pre):
@@ -55,15 +63,21 @@
 
 
 def edge_tables():
-    place_fine = np.zeros((3, 16, LANES), np.float32)
-    place_coarse = np.zeros((3, 16, LANES), np.float32)
-    for a in range(3):
-        for base, start in ((0, 0), (8, 64)):
-            for r in range(4):
-                place_fine[a, base + r + a, start + r] = 1
-            for r in range(2):
-                place_coarse[a, base + (0, 1, 3, 5)[r + a], start + r] = 1
-    return place_fine, place_coarse
+    place = np.zeros((4, 16, LANES), np.float32)
+    for r in range(4):
+        for side in range(2):
+            for a in range(3):
+                place[a, 8 * side + r + a, fine_lanes(r)[side]] = 1
+            place[3, 8 * side + (0, 1, 3, 5)[r], coarse_lanes(r - 1)[side]] = 1
+    panel = np.zeros((9, 32, LANES), np.float32)
+    for side in range(2):
+        for row in range(-3, 7):
+            for c in range(6):
+                df = -1 if row < 0 else int(row > 3)
+                dt = (-1 if c < 3 else 0) if side == 0 else int(c >= 3)
+                source = 8 if (df, dt) == (0, 0) else DIRS.index((df, dt))
+                panel[source, 8 * (row - 4 * df) + (c + 3) % 6, 64 * side + PITCH * (row + 3) + c] = 1
+    return place, panel.reshape(288, LANES)
 
 
 def first_tables():
@@ -78,7 +92,7 @@
     return (tables,)
 
 
-def conv_rows(weight, x_ref, outs, rows, step):
+def conv_rows(weight, x_ref, outs, rows, step, halo_lanes):
     z = jnp.dot(weight, x_ref[...], preferred_element_type=F32)
     lane = lanes_of(outs)
     halo_left = z[:outs, rows * LANES :]
@@ -86,15 +100,21 @@
     result = []
     for r in range(rows):
         at = slice(r * LANES, (r + 1) * LANES)
-        left = jnp.where(lane < step, halo_left[:, r : r + 1], roll(z[:outs, at], step))
+        on_left, on_right = halo_lanes(r)
+        left = jnp.where(
+            lane < step, halo_left[:, on_left : on_left + 1], roll(z[:outs, at], step)
+        )
         right = jnp.where(
-            lane >= LANES - step, halo_right[:, 64 + r : 65 + r], roll(z[2 * outs :, at], -step)
+            lane >= LANES - step,
+            halo_right[:, on_right : on_right + 1],
+            roll(z[2 * outs :, at], -step),
         )
         result.append(z[outs : 2 * outs, at] + left + right)
-    return result
-
-
-def weight_grad(delta_rows, x_ref, step):
+    panel = z[outs : 2 * outs, rows * LANES :] + roll(halo_left, 1) + roll(halo_right, -1)
+    return result, panel
+
+
+def weight_grad(delta_rows, field, step, halo_lanes):
     outs = delta_rows[0].shape[0]
     lane = lanes_of(outs)
     keep = (lane & (step - 1)) == 0
@@ -105,14 +125,15 @@
         first.append(jnp.where(keep & (lane < LANES - step), roll(delta, -step), 0.0))
         middle.append(jnp.where(keep, delta, 0.0))
         last.append(jnp.where(keep & (lane >= step), roll(delta, step), 0.0))
-        halo_left = jnp.where(lane == r, delta[:, 0:1], halo_left)
-        halo_right = jnp.where(lane == 64 + r, delta[:, LANES - 1 : LANES], halo_right)
+        on_left, on_right = halo_lanes(r)
+        halo_left = jnp.where(lane == on_left, delta[:, 0:1], halo_left)
+        halo_right = jnp.where(lane == on_right, delta[:, LANES - 1 : LANES], halo_right)
     parts = [first + [halo_left], middle + [zero], last + [halo_right]]
     stacked = jnp.concatenate(
         [jnp.concatenate(part, axis=1).astype(BF) for part in parts], axis=0
     )
     return lax.dot_general(
-        stacked, x_ref[...], (((1,), (1,)), ((), ())), preferred_element_type=F32
+        stacked, field, (((1,), (1,)), ((), ())), preferred_element_type=F32
     )
 
 
@@ -134,8 +155,8 @@
     w3_hbm,
     wo_hbm,
     find_hbm,
-    placef_hbm,
-    placec_hbm,
+    place_hbm,
+    panel_hbm,
     pred_ref,
     gfirst_ref,
     gdown_ref,
@@ -153,8 +174,8 @@
     w3_ref,
     wo_ref,
     find_ref,
-    placef_ref,
-    placec_ref,
+    place_ref,
+    panel_ref,
     load_sem,
     s1,
     s2,
@@ -173,6 +194,10 @@
     row_recv,
     edge_send,
     edge_recv,
+    wide_own,
+    wide_recv,
+    rim_send,
+    rim_recv,
     x1,
     x2,
     x3,
@@ -200,6 +225,8 @@
     box_rsem,
     ex_ssem,
     ex_rsem,
+    wide_ssem,
+    wide_rsem,
     xy_ssem,
     xy_rsem,
     zs_ssem,
@@ -253,18 +280,11 @@
                 (interp_hbm, interp_ref),
                 (sea_hbm, sea_ref),
                 (cot_hbm, cot_ref),
-                (placef_hbm, placef_ref),
-                (placec_hbm, placec_ref),
+                (place_hbm, place_ref),
+                (panel_hbm, panel_ref),
             )
         )
     ]
-    for load in loads:
-        load.start()
-
-    row_recv[...] = jnp.zeros_like(row_recv)
-    edge_recv[...] = jnp.zeros_like(edge_recv)
-    edge_send[...] = jnp.zeros_like(edge_send)
-
     barrier = pltpu.get_barrier_semaphore()
 
     def greet(peer, count):
@@ -274,7 +294,14 @@
 
         lax.fori_loop(count[0], count[1], body, 0)
 
-    greet(box_peer, (0, nt))
+    far_first = sorted(range(nt), key=lambda k: -min(k % nz, nz - k % nz))
+    for k in far_first:
+        pl.semaphore_signal(barrier, inc=1, device_id=box_peer(k)[1], device_id_type=MESH)
+    row_recv[...] = jnp.zeros_like(row_recv)
+    edge_recv[...] = jnp.zeros_like(edge_recv)
+    wide_recv[...] = jnp.zeros_like(wide_recv)
+    rim_recv[...] = jnp.zeros_like(rim_recv)
+    rim_send[...] = jnp.zeros_like(rim_send)
     greet(xy_peer, (1, nxy))
     greet(z_peer, (1, nz))
     expected = nt + nxy - 1 + nz - 1
@@ -285,6 +312,9 @@
         @pl.when(ok)
         def _(device=device):
             pl.semaphore_signal(barrier, inc=1, device_id=device, device_id_type=MESH)
+
+    for load in loads:
+        load.start()
 
     rows = 2 * nt * KC
     nblk = src_ref.shape[1]
@@ -387,7 +417,8 @@
 
         lax.fori_loop(low, high, body, 0)
 
-    each(0, nt, lambda k: box_copy(k).start())
+    for k in far_first:
+        box_copy(k).start()
 
     for load in loads[4:]:
         load.wait()
@@ -462,8 +493,8 @@
         ok, device = neighbour(d)
         at = d if arrival else OPP[d]
         if d < 2:
-            src = row_send.at[e, d, 0 : EX_CH[e]]
-            dst = row_recv.at[e, at, 0 : EX_CH[e]]
+            src = row_send.at[e, d]
+            dst = row_recv.at[e, at]
         else:
             src = edge_send.at[e]
             dst = edge_recv.at[e, at - 2]
@@ -476,19 +507,40 @@
             device_id_type=MESH,
         )
 
-    def ex_start(e):
-        for d in range(8):
-            ok, copy = ex_copy(e, d, False)
+    def wide_copy(e, i, arrival):
+        d = i if i < 8 else i - 8
+        ok, device = neighbour(d)
+        at = d if arrival else OPP[d]
+        if i >= 8:
+            src = wide_own.at[e, 0 : WIDE_CH[e], LANES * d : LANES * d + 3 * LANES]
+            dst = wide_recv.at[e, at, 0 : WIDE_CH[e]]
+        else:
+            src = rim_send.at[e]
+            dst = rim_recv.at[e, at]
+        return ok, pltpu.make_async_remote_copy(
+            src_ref=src,
+            dst_ref=dst,
+            send_sem=wide_ssem.at[e, i],
+            recv_sem=wide_rsem.at[e, at if i < 8 else 8 + at],
+            device_id=device,
+            device_id_type=MESH,
+        )
+
+    def start_all(copy_of, e, count):
+        for d in reversed(range(count)):
+            ok, copy = copy_of(e, d, False)
             pl.when(ok)(copy.start)
 
-    def ex_wait(e):
-        for d in range(8):
-            ok, copy = ex_copy(e, d, True)
+    def wait_all(copy_of, e, count):
+        for d in range(count):
+            ok, copy = copy_of(e, d, True)
 
             @pl.when(ok)
             def _(copy=copy):
                 copy.wait_recv()
                 copy.wait_send()
+
+    lane16 = lanes_of(16)
 
     def edge_pick(rows_of):
         parts = []
@@ -500,9 +552,16 @@
             parts.append(jnp.where(hit, 1.0, 0.0))
         return jnp.concatenate(parts, axis=1).astype(BF)
 
-    lane16 = lanes_of(16)
-    pick_fine = edge_pick(((1, 5), (2,), (3,), (0, 4)))
     pick_coarse = edge_pick(((1, 2, 5), (0, 3, 4)))
+    sub32 = lax.broadcasted_iota(jnp.int32, (32, LANES), 0)
+    lane32 = lanes_of(32)
+    column = sub32 & 7
+    on_edge = ((column < 3) & (lane32 == column)) | (
+        (column >= 3) & (column < 6) & (lane32 == LANES - 6 + column)
+    )
+    pick_rim = jnp.concatenate(
+        [jnp.where(on_edge & ((sub32 >> 3) == r), 1.0, 0.0) for r in range(4)], axis=1
+    ).astype(BF)
 
     def pick(table, field):
         return lax.dot_general(
@@ -522,32 +581,52 @@
         held = jnp.zeros((16, LANES), F32)
         for d in range(2, 8):
             held = jnp.where(takes[d], edge_recv[e, d - 2].astype(F32), held)
-        return held.T
-
-    def place(columns, table_ref, a):
-        return jnp.dot(
-            columns.astype(BF), table_ref[a], preferred_element_type=F32
-        ).astype(BF)
-
-    def fill_centre(x_ref, chans, offset, total, field_rows):
-        count = len(field_rows)
+        return held.astype(BF)
+
+    def place(columns, table):
+        return lax.dot_general(
+            columns, table, (((0,), (0,)), ((), ())), preferred_element_type=F32
+        )
+
+    def wide_start(e, own_rows):
+        flat = jnp.concatenate(own_rows, axis=1)
+        wide_own[e, 0 : WIDE_CH[e]] = flat
+        rim_send[e, :, 0 : WIDE_CH[e]] = pick(pick_rim, flat)
+        start_all(wide_copy, e, 10)
+
+    def wide_finish(e, own_rows):
+        wait_all(wide_copy, e, 10)
+        rims = jnp.concatenate([rim_recv[e, d] for d in range(8)] + [rim_send[e]], axis=0)
+        panel = place(rims, panel_ref[...])[0 : WIDE_CH[e]]
+        above = [wide_recv[e, 0, 0 : WIDE_CH[e], LANES * r : LANES * r + LANES] for r in range(3)]
+        below = [wide_recv[e, 1, 0 : WIDE_CH[e], LANES * r : LANES * r + LANES] for r in range(3)]
+        return above + own_rows + below, panel
+
+    def fill(x_ref, chans, offset, total, ext_rows, panel, row_lanes):
+        count = len(ext_rows) - 2
         for a in range(3):
+            at = slice(a * total + offset, a * total + offset + chans)
             for r in range(count):
-                if 1 <= r + a <= count:
-                    x_ref[
-                        a * total + offset : a * total + offset + chans,
-                        r * LANES : (r + 1) * LANES,
-                    ] = field_rows[r + a - 1]
-
-    def fill_halo(x_ref, chans, offset, total, count, above, below, columns, table_ref):
-        x_ref[offset : offset + chans, 0:LANES] = above
-        x_ref[
-            2 * total + offset : 2 * total + offset + chans, (count - 1) * LANES : count * LANES
-        ] = below
-        for a in range(3):
-            x_ref[
-                a * total + offset : a * total + offset + chans, count * LANES :
-            ] = place(columns, table_ref, a)
+                if ext_rows[r + a] is not None:
+                    x_ref[at, r * LANES : (r + 1) * LANES] = ext_rows[r + a]
+            if panel is not None:
+                moved = roll(panel, (1 - a) * row_lanes) if a != 1 else panel
+                x_ref[at, count * LANES :] = moved.astype(BF)
+
+    side_lane = lanes_of(CH) & 63
+    panel_row = ((side_lane * 43) >> 8) - 3
+    panel_col = side_lane - (panel_row + 3) * PITCH
+    on_right_side = lanes_of(CH) >= 64
+    row_low = jnp.where(face > 0, -3, 0)
+    row_high = jnp.where(face < nf - 1, 6, 3)
+    left_low = jnp.where(tile > 0, 0, 3)
+    right_high = jnp.where(tile < nt - 1, 5, 2)
+    in_grid = (
+        (panel_row >= row_low)
+        & (panel_row <= row_high)
+        & (on_right_side | (panel_col >= left_low))
+        & (~on_right_side | (panel_col <= right_high))
+    )
 
     groups = (
         (na, send_a, recv_a, part_a, zrecv_a, done_a, all_a, 0),
@@ -724,77 +803,58 @@
             jnp.concatenate([state_rows[q].astype(BF), forcing], axis=0)
         )
 
-    row_send[0, 0, 0:32] = lifted[0]
-    row_send[0, 1, 0:32] = lifted[3]
-    edge_send[0, :, 0:32] = pick(pick_fine, jnp.concatenate(lifted, axis=1))
-    ex_start(0)
-    fill_centre(x1, 32, 0, 32, lifted)
-    ex_wait(0)
-    columns = halo_columns(0)[0:32]
-    fill_halo(
-        x1, 32, 0, 32, 4, row_recv[0, 0, 0:32], row_recv[0, 1, 0:32], columns, placef_ref
-    )
-    pre = conv_rows(a1[...], x1, CH, 4, 1)
+    wide_start(0, lifted)
+    ext, panel = wide_finish(0, lifted)
+    fill(x1, 32, 0, 32, ext, panel, PITCH)
+    pre, pre_panel = conv_rows(a1[...], x1, CH, 8, 1, lambda r: fine_lanes(r - 2))
     hidden_one, slope_one = [], []
-    for r in range(4):
+    for r in range(8):
         value, slope = gelu_pair(pre[r])
+        if r < 2:
+            value = jnp.where(face > 0, value, 0.0)
+        elif r >= 6:
+            value = jnp.where(face < nf - 1, value, 0.0)
+        else:
+            slope_one.append(slope)
         hidden_one.append(value.astype(BF))
-        slope_one.append(slope)
+    one_panel = jnp.where(in_grid, gelu_pair(pre_panel)[0], 0.0).astype(BF).astype(F32)
+
     pooled = [
         (
             pair_sum(hidden_one[2 * r].astype(F32) + hidden_one[2 * r + 1].astype(F32)) * 0.25
         ).astype(BF)
-        for r in range(2)
+        for r in range(4)
     ]
 
-    for at, fine, coarse in ((0, 0, 0), (1, 3, 1)):
-        row_send[1, at, 0:CH] = hidden_one[fine]
-        row_send[1, at, CH : 2 * CH] = pooled[coarse]
-    edge_send[1] = jnp.concatenate(
-        [
-            pick(pick_fine, jnp.concatenate(hidden_one, axis=1)),
-            pick(pick_coarse, jnp.concatenate(pooled, axis=1)),
-        ],
-        axis=1,
-    )
-    ex_start(1)
-    fill_centre(x3, CH, 0, 3 * CH, hidden_one)
-    fill_centre(x2, CH, 0, CH, pooled)
-    ex_wait(1)
-    columns = halo_columns(1)
-    fill_halo(
-        x2,
-        CH,
-        0,
-        CH,
-        2,
-        row_recv[1, 0, CH : 2 * CH],
-        row_recv[1, 1, CH : 2 * CH],
-        columns[CH : 2 * CH],
-        placec_ref,
-    )
-    pre = conv_rows(a2[...], x2, 2 * CH, 2, 2)
+    def panel_sum(field):
+        field = field + roll(field, -1)
+        return field + roll(field, -PITCH)
+
+    fill(x2, CH, 0, CH, pooled, panel_sum(one_panel) * 0.25, 2 * PITCH)
+    pre, _ = conv_rows(a2[...], x2, 2 * CH, 2, 2, coarse_lanes)
     hidden_two, slope_two = [], []
     for r in range(2):
         value, slope = gelu_pair(pre[r])
         hidden_two.append(value.astype(BF))
         slope_two.append(slope)
 
-    row_send[2, 0] = hidden_two[0]
-    row_send[2, 1] = hidden_two[1]
-    edge_send[2] = pick(pick_coarse, jnp.concatenate(hidden_two, axis=1))
-    ex_start(2)
-    fill_halo(
-        x3, CH, 0, 3 * CH, 4, row_recv[1, 0, 0:CH], row_recv[1, 1, 0:CH], columns[0:CH], placef_ref
-    )
-    fill_centre(x3, 2 * CH, CH, 3 * CH, [hidden_two[r // 2] for r in range(4)])
+    for e, field in ((0, hidden_two), (1, [slope.astype(BF) for slope in slope_two])):
+        row_send[e, 0] = field[0]
+        row_send[e, 1] = field[1]
+        edge_send[e] = pick(pick_coarse, jnp.concatenate(field, axis=1))
+        start_all(ex_copy, e, 8)
+    fill(x3, CH, 0, 3 * CH, hidden_one[1:7], one_panel, PITCH)
+    fill(x3, 2 * CH, CH, 3 * CH, [None] + [hidden_two[r // 2] for r in range(4)] + [None], None, 0)
     back_three = jnp.dot(wot, cot, preferred_element_type=F32)
-    ex_wait(2)
-    columns = halo_columns(2)
-    fill_halo(
-        x3, 2 * CH, CH, 3 * CH, 4, row_recv[2, 0], row_recv[2, 1], columns, placef_ref
-    )
-    pre = conv_rows(a3[...], x3, CH, 4, 1)
+    wait_all(ex_copy, 0, 8)
+    columns = halo_columns(0)
+    x3[CH : 3 * CH, 0:LANES] = row_recv[0, 0]
+    x3[7 * CH : 9 * CH, 3 * LANES : 4 * LANES] = row_recv[0, 1]
+    for a in range(3):
+        x3[3 * CH * a + CH : 3 * CH * a + 3 * CH, 4 * LANES :] = place(
+            columns, place_ref[a]
+        ).astype(BF)
+    pre, _ = conv_rows(a3[...], x3, CH, 4, 1, fine_lanes)
     hidden_three, delta_three = [], []
     for r in range(4):
         value, slope = gelu_pair(pre[r])
@@ -803,11 +863,7 @@
             (back_three[:, r * LANES : (r + 1) * LANES] * slope).astype(BF)
         )
 
-    row_send[3, 0, 0:CH] = delta_three[0]
-    row_send[3, 1, 0:CH] = delta_three[3]
-    edge_send[3, :, 0:CH] = pick(pick_fine, jnp.concatenate(delta_three, axis=1))
-    ex_start(3)
-    fill_centre(xd3, CH, 0, CH, delta_three)
+    wide_start(1, delta_three)
     flat_three = jnp.concatenate(hidden_three, axis=1)
     change = jnp.dot(wo, flat_three, preferred_element_type=F32)
     for r in range(4):
@@ -816,7 +872,7 @@
     grad_out = lax.dot_general(
         cot, flat_three, (((1,), (1,)), ((), ())), preferred_element_type=F32
     )
-    grad_up = weight_grad([d.astype(F32) for d in delta_three], x3, 1)
+    grad_up = weight_grad([d.astype(F32) for d in delta_three], x3[...], 1, fine_lanes)
     tiles = [grad_up[:, LANES * t : LANES * t + LANES] for t in range(4)]
     tiles.append(jnp.concatenate([grad_up[:, 512:576], jnp.zeros((192, CH), F32)], axis=1))
     lane_up = lanes_of(192)
@@ -846,23 +902,21 @@
     if 16 * na * nxy > 880:
         send_a[880:] = jnp.zeros((16 * na * nxy - 880, LANES), BF)
     xy_start(0)
-    ex_wait(3)
-    columns = halo_columns(3)[0:CH]
-    fill_halo(
-        xd3, CH, 0, CH, 4, row_recv[3, 0, 0:CH], row_recv[3, 1, 0:CH], columns, placef_ref
-    )
-    join = conv_rows(b3[...], xd3, 3 * CH, 4, 1)
+    wait_all(ex_copy, 1, 8)
+    ext, panel = wide_finish(1, delta_three)
+    fill(xd3, CH, 0, CH, ext, panel, PITCH)
+    join, join_panel = conv_rows(b3[...], xd3, 3 * CH, 8, 1, lambda r: fine_lanes(r - 2))
+    slopes = [row_recv[1, 0].astype(F32)] + slope_two + [row_recv[1, 1].astype(F32)]
     delta_two = [
-        (pair_sum(join[2 * r][CH:] + join[2 * r + 1][CH:]) * slope_two[r]).astype(BF)
-        for r in range(2)
+        (pair_sum(join[2 * r][CH:] + join[2 * r + 1][CH:]) * slopes[r]).astype(BF)
+        for r in range(4)
     ]
-
-    row_send[4, 0] = delta_two[0]
-    row_send[4, 1] = delta_two[1]
-    edge_send[4] = pick(pick_coarse, jnp.concatenate(delta_two, axis=1))
-    ex_start(4)
-    fill_centre(xd2, 2 * CH, 0, 2 * CH, delta_two)
-    grad_down = weight_grad([d.astype(F32) for d in delta_two], x2, 2)
+    two_panel = (
+        (panel_sum(join_panel[CH:]) * place(halo_columns(1), place_ref[3])).astype(BF).astype(F32)
+    )
+
+    fill(xd2, 2 * CH, 0, 2 * CH, delta_two, two_panel, 2 * PITCH)
+    grad_down = weight_grad([d.astype(F32) for d in delta_two[1:3]], x2[...], 2, coarse_lanes)
     lane_down = lanes_of(CH)
     right = jnp.concatenate([grad_down[:, 128:192], jnp.zeros((384, CH), F32)], axis=1)
     for b in range(3):
@@ -881,25 +935,25 @@
     if 16 * nb * nxy > 576:
         send_b[576:] = jnp.zeros((16 * nb * nxy - 576, LANES), BF)
     xy_start(1)
-    stage_xy_to_z(0)
-    ex_wait(4)
-    columns = halo_columns(4)
-    fill_halo(
-        xd2, 2 * CH, 0, 2 * CH, 2, row_recv[4, 0], row_recv[4, 1], columns, placec_ref
-    )
-    d_pool = conv_rows(b2[...], xd2, CH, 2, 2)
+    d_pool, _ = conv_rows(b2[...], xd2, CH, 2, 2, coarse_lanes)
     delta_one = [
-        ((join[r][0:CH] + 0.25 * d_pool[r // 2]) * slope_one[r]).astype(BF).astype(F32)
+        ((join[2 + r][0:CH] + 0.25 * d_pool[r // 2]) * slope_one[r]).astype(BF).astype(F32)
         for r in range(4)
     ]
-    grad_first = weight_grad(delta_one, x1, 1)
+    grad_first = weight_grad(
+        delta_one,
+        jnp.concatenate([x1[:, 2 * LANES : 6 * LANES], x1[:, 8 * LANES :]], axis=1),
+        1,
+        fine_lanes,
+    )
     send_c[0:192] = jnp.concatenate([grad_first, jnp.zeros((192, 32), F32)], axis=1).astype(BF)
     if 16 * nc * nxy > 192:
         send_c[192:] = jnp.zeros((16 * nc * nxy - 192, LANES), BF)
     xy_start(2)
+    stage_xy_to_z(0)
     stage_xy_to_z(1)
+    stage_xy_to_z(2)
     stage_z_reduce(0)
-    stage_xy_to_z(2)
     stage_z_reduce(1)
     stage_z_to_xy(0)
     stage_all_z()
@@ -909,21 +963,12 @@
     for t in range(3):
         for k in range(9):
             at = 32 * (9 * t + k)
-            part = all_a[at : at + 32].astype(F32) * scale
-            if k < 8:
-                s3[t, pl.ds(k, CH // 2, stride=8), :] = part
-            else:
-                s3[t, 256:288] = part
-    for j in range(CH // 2):
-        for t in range(3):
-            at = 384 * j + 128 * t
-            gup_ref[0:8, at : at + 128] = s3[t, 8 * j : 8 * j + 8]
-            gup_ref[8:9, at : at + 128] = s3[t, 256 + j : 257 + j]
+            gup_ref[k, pl.ds(t, CH // 2, stride=3), :] = all_a[at : at + 32].astype(F32) * scale
     part = all_a[864:880].astype(F32) * scale
     turned = roll(part, CH)
     lane1 = lanes_of(1)
     for j in range(CIN // 2):
-        gout_ref[0:1, LANES * j : LANES * j + LANES] = jnp.where(
+        gout_ref[j : j + 1] = jnp.where(
             lane1 < CH, part[2 * j : 2 * j + 1], turned[2 * j + 1 : 2 * j + 2]
         )
     stage_finish(2)
@@ -946,19 +991,12 @@
         )
         for step in range(2)
     )
-    for j in range(10):
-        gfirst_ref[0:8, 128 * j : 128 * j + 128] = flat_first[8 * j : 8 * j + 8] * scale
-        gfirst_ref[8:9, 128 * j : 128 * j + 128] = flat_first[80 + j : 81 + j] * scale
+    s1[...] = flat_first * scale
+    for k in range(9):
+        gfirst_ref[k] = s1[pl.ds(k, 10, stride=8), :] if k < 8 else s1[80:90]
     stage_finish(1)
     for k in range(9):
-        part = all_b[CH * k : CH * k + CH].astype(F32) * scale
-        if k < 8:
-            s2[pl.ds(k, CH, stride=8), :] = part
-        else:
-            s2[512:576] = part
-    for j in range(CH):
-        gdown_ref[0:8, 128 * j : 128 * j + 128] = s2[8 * j : 8 * j + 8]
-        gdown_ref[8:9, 128 * j : 128 * j + 128] = s2[512 + j : 513 + j]
+        gdown_ref[k] = all_b[CH * k : CH * k + CH].astype(F32) * scale
     each(0, nt, lambda k: box_copy(k).wait_send())
 
 
@@ -1012,14 +1050,18 @@
         pltpu.VMEM((9 * CH, 3 * CH), BF),
         pltpu.VMEM((nt, KC, LANES), F32),
         pltpu.VMEM((nt, KC, LANES), F32),
-        pltpu.VMEM((N_EX, 2, LANES, LANES), BF),
-        pltpu.VMEM((N_EX, 2, LANES, LANES), BF),
-        pltpu.VMEM((N_EX, 16, LANES), BF),
-        pltpu.VMEM((N_EX, 6, 16, LANES), BF),
-        pltpu.VMEM((96, 5 * LANES), BF),
+        pltpu.VMEM((2, 2, LANES, LANES), BF),
+        pltpu.VMEM((2, 2, LANES, LANES), BF),
+        pltpu.VMEM((2, 16, LANES), BF),
+        pltpu.VMEM((2, 6, 16, LANES), BF),
+        pltpu.VMEM((2, CH, 4 * LANES), BF),
+        pltpu.VMEM((2, 2, CH, 3 * LANES), BF),
+        pltpu.VMEM((2, 32, LANES), BF),
+        pltpu.VMEM((2, 8, 32, LANES), BF),
+        pltpu.VMEM((96, 9 * LANES), BF),
         pltpu.VMEM((3 * CH, 3 * LANES), BF),
         pltpu.VMEM((9 * CH, 5 * LANES), BF),
-        pltpu.VMEM((3 * CH, 5 * LANES), BF),
+        pltpu.VMEM((3 * CH, 9 * LANES), BF),
         pltpu.VMEM((6 * CH, 3 * LANES), BF),
     ]
     for n in (na, nb, nc):
@@ -1034,8 +1076,10 @@
     scratch += [
         dma((nt,)),
         dma((nt,)),
-        dma((N_EX, 8)),
-        dma((N_EX, 8)),
+        dma((2, 8)),
+        dma((2, 8)),
+        dma((2, 10)),
+        dma((2, 10)),
         dma((3, nxy)),
         dma((3, nxy)),
         dma((na + nb,)),
@@ -1052,10 +1096,10 @@
         functools.partial(kernel, nf, nt, na, nb, nc),
         out_shape=(
             jax.ShapeDtypeStruct((CIN, 4, LANES), BF),
-            jax.ShapeDtypeStruct(w_first.shape[1:], F32),
-            jax.ShapeDtypeStruct(w_down.shape[1:], F32),
-            jax.ShapeDtypeStruct(w_up.shape[1:], F32),
-            jax.ShapeDtypeStruct(w_out.shape, F32),
+            jax.ShapeDtypeStruct((9, 10, LANES), F32),
+            jax.ShapeDtypeStruct((9, 64, LANES), F32),
+            jax.ShapeDtypeStruct((9, 96, LANES), F32),
+            jax.ShapeDtypeStruct((8, LANES), F32),
         ),
         in_specs=[pl.BlockSpec(memory_space=pltpu.HBM)] * len(operands),
         out_specs=(vmem,) * 5,
@@ -1065,7 +1109,13 @@
         ),
     )(*operands)
 
-    return predicted[None], grad_first[None], grad_down[None], grad_up[None], grad_out
+    return (
+        predicted[None],
+        grad_first.reshape(1, 9, -1),
+        grad_down.reshape(1, 9, -1),
+        grad_up.reshape(1, 9, -1),
+        grad_out.reshape(1, -1),
+    )
 
 
 def solution(mesh):

time: 87.4 us -> 83.3 us (0.953)
  the two profiles are of different devices: /device:TPU:8 before, /device:TPU:4 now
where the time goes in v4:
time: 83.3 us; the launch traced here: 83 us
  Pallas kernels  76.4 us (92%)
  local copies, waits for them, and re-layouts  5.99 us (7%)
    pallas_call x1, Pallas kernels, local(): pl.pallas_call(functools.partial(kernel, nf, nt, na, nb, nc), out_shape=(...  76.4 us
    unnamed x8, local copies, waits for them, and re-layouts  4.38 us

profile of v4, /device:TPU:4, one launch (start us, length us, event | category | flops | bytes accessed | tf_op | source)
XLA Modules:
  0.0 83.0 jit_solution(12485172761453598088)
XLA Ops:
  0.6 76.4 %shard_map.173 = (bf16[16,4,128]{2,1,0:T(4,128)(2,1)}, f32[9,10,128]{2,1,0:T(8,128)}, f32[9,64,128]{2,1,0:T(8,128)}, f32[9,96,128]{2,1,0:T(8,128)}, f32[8,128]{1,0:T(8,128)}) custom-call(bf16[16,4,128]{2,1,0:T(4,128)(2,1)} %bitcast.21, bf16[16,4,128]{2,1,0:T(4,128)(2,1)} %bitcast.22, s32[1,32]{1,0:T(1,128)} %bitcast.28, s32[1,32]{1,0:T(1,128)} %bitcast.29, ...), custom_call_target="tpu_custom_call" | custom-call | tf_op jit(solution)/shard_map/pallas_call | solution.py:1095
  77.0 0.0 copy-start
  77.1 1.6 %reshape.38 = f32[1,9,1280]{2,0,1:T(1,128)} reshape(f32[9,10,128]{2,1,0:T(8,128)} %get-tuple-element.11) | data formatting | bytes 92160 | tf_op jit(solution)/shard_map/reshape | solution.py:1114
  78.7 1.3 %copy.29 = bf16[1,16,4,128]{3,2,1,0:T(4,128)(2,1)} copy(bf16[1,16,4,128]{3,2,1,0:T(4,128)(2,1)} %bitcast.24) | data formatting | bytes 32768
  80.0 1.7 %copy.30 = f32[1,9,8192]{2,0,1:T(1,128)} copy(f32[1,9,8192]{2,0,1:T(1,128)} %bitcast.18) | data formatting | bytes 589824
  81.7 0.0 copy-done
  81.7 0.0 copy-start.1
  81.7 0.8 copy.31
  82.4 0.0 copy-done.1
  82.4 0.6 copy.32
Async XLA Ops:
  77.0 4.6 %copy-start = (f32[9,96,128]{2,1,0:T(8,128)S(1)}, f32[9,96,128]{2,1,0:T(8,128)}, u32[]{:S(2)}) copy-start(f32[9,96,128]{2,1,0:T(8,128)} %get-tuple-element.13) | copy-start | bytes 1327108
  81.7 0.8 copy-start.1
